TPU v7x, 32 devices: a whole 2x2x4 slice. The times are simulated.
32 devices in a mesh: wide: 8 (over z, y), narrow: 4 (over x, core).
Axes of the slice: x: 2, y: 2, z: 4, core: 2. Of those that a mesh axis runs over, the one named last changes fastest.
Arguments:
- queries: bfloat16 [16, 128, 2304], P('wide'), may hold values from -112 to 112
- new_kv: bfloat16 [16, 2, 128, 2304], P('wide', None, 'narrow'), may hold values from -4 to 4
- cache_pool: bfloat16 [16, 16, 2, 128, 2304], P('wide', 'narrow'), may hold values from -4 to 4
- page_table: int32 [16, 16], P('wide'), may hold values from 0 to 15, as said below
- cached_len: int32 [16], P('wide'), may hold values from 0 to 2048, as said below
- residual: bfloat16 [2048, 2304], P('wide'), may hold values from -0.1796875 to 0.1796875
- norm_gain: float32 [2304], replicated, may hold values from 0.1 to 1.9
- expert_ids: int32 [2048, 2], P('wide'), may hold values from 0 to 7, all different within a row; in each aligned block of 256 rows (0 to 255, 256 to 511, ...) at most 80 rows name the same one
- route_weight: float32 [2048, 2], P('wide'), may hold values from 0.1 to 1
- w_gate_up: bfloat16 [8, 2304, 2, 5760], P(None, 'narrow', None, 'wide'), may hold values from -0.125 to 0.125
- w_down: bfloat16 [8, 5760, 2304], P(None, 'wide', 'narrow'), may hold values from -0.078125 to 0.078125
Outputs:
- layer_out: bfloat16 [2048, 2304], P('wide', 'narrow')
Inputs may be any that keep to these rules, and one draw needn't show every extreme that they name: `page_table`: for each request the 16 entries are distinct, and entry j lies in (j % 4) * 4 to (j % 4) * 4 + 3. `cached_len`: some request has exactly 2048 cached tokens. `expert_ids`: A token's two experts differ; among the 256 tokens of one index of wide no expert is named more than 80 times.
All inputs are finite; a program needn't handle non-finite values.
Results may differ from a plain program's by a relative error of at most 0.035.
Values may be sent and summed in bfloat16 or wider, within the bound.
A program may use at most 192 MiB of HBM per device.

v0:
```python
import jax
import jax.numpy as jnp
from jax import lax
from jax.sharding import PartitionSpec as P

HD = 64
CAP = 80


NEG_FILL = -1e30
SCORE_SCALE = 0.125
EPSILON = 1e-05


def activate(gate_up, unit_count):
    return (jax.nn.silu(gate_up[..., :unit_count]) * gate_up[..., unit_count:]).astype(jnp.bfloat16)


def local(
    queries,
    new_kv,
    cache_pool,
    page_table,
    cached_len,
    residual,
    norm_gain,
    expert_ids,
    route_weight,
    w_gate_up,
    w_down,
):
    narrow_count = lax.axis_size("narrow")
    narrow_pos = lax.axis_index("narrow")
    wide_count = lax.axis_size("wide")
    req_here, new_len, model_width = queries.shape
    head_count = model_width // HD
    slot_count = cache_pool.shape[1]
    page_len = cache_pool.shape[3]
    local_new = new_kv.shape[2]
    table_len = page_table.shape[1]
    query_heads = queries.reshape(req_here, new_len, head_count, HD)
    cache_keys = cache_pool[:, :, 0].reshape(req_here, slot_count * page_len, head_count, HD)
    cache_vals = cache_pool[:, :, 1].reshape(req_here, slot_count * page_len, head_count, HD)
    new_keys = new_kv[:, 0].reshape(req_here, local_new, head_count, HD)
    new_vals = new_kv[:, 1].reshape(req_here, local_new, head_count, HD)
    own_slots = narrow_pos * slot_count + jnp.arange(slot_count, dtype=jnp.int32)
    matches = page_table[:, None, :] == own_slots[None, :, None]
    logical = jnp.sum(
        jnp.where(matches, jnp.arange(table_len, dtype=jnp.int32)[None, None, :], 0), axis=2
    )
    key_pos = logical[:, :, None] * page_len + jnp.arange(page_len, dtype=jnp.int32)[None, None, :]
    cache_valid = key_pos.reshape(req_here, slot_count * page_len) < cached_len[:, None]
    new_pos = narrow_pos * local_new + jnp.arange(local_new, dtype=jnp.int32)
    new_valid = new_pos[None, :] <= jnp.arange(new_len, dtype=jnp.int32)[:, None]
    cache_scores = (
        jnp.einsum("rqhd,rkhd->rhqk", query_heads, cache_keys, preferred_element_type=jnp.float32)
        * SCORE_SCALE
    )
    new_scores = (
        jnp.einsum("rqhd,rkhd->rhqk", query_heads, new_keys, preferred_element_type=jnp.float32)
        * SCORE_SCALE
    )
    cache_scores = jnp.where(cache_valid[:, None, None, :], cache_scores, NEG_FILL)
    new_scores = jnp.where(new_valid[None, None], new_scores, NEG_FILL)
    local_top = jnp.maximum(jnp.max(cache_scores, axis=3), jnp.max(new_scores, axis=3))
    score_top = lax.pmax(local_top.astype(jnp.bfloat16), "narrow").astype(local_top.dtype)
    cache_weights = jnp.where(
        cache_valid[:, None, None, :], jnp.exp(cache_scores - score_top[..., None]), 0.0
    )
    new_weights = jnp.where(new_valid[None, None], jnp.exp(new_scores - score_top[..., None]), 0.0)
    denominator = jnp.sum(cache_weights, axis=3) + jnp.sum(new_weights, axis=3)
    numerator = jnp.einsum(
        "rhqk,rkhd->rqhd",
        cache_weights.astype(jnp.bfloat16),
        cache_vals,
        preferred_element_type=jnp.float32,
    )
    numerator = numerator + jnp.einsum(
        "rhqk,rkhd->rqhd",
        new_weights.astype(jnp.bfloat16),
        new_vals,
        preferred_element_type=jnp.float32,
    )
    total_num, total_den = (
        lax.psum(
            numerator.reshape(req_here, new_len, model_width).astype(jnp.bfloat16), "narrow"
        ).astype(jnp.float32),
        lax.psum(denominator.astype(jnp.bfloat16), "narrow").astype(jnp.float32),
    )
    attention = (
        total_num.reshape(req_here, new_len, head_count, HD)
        / jnp.transpose(total_den, (0, 2, 1))[..., None]
    )
    hidden = residual.astype(jnp.float32) + attention.reshape(req_here * new_len, model_width)
    spread = jnp.mean(hidden * hidden, axis=1, keepdims=True)
    normed = (hidden * lax.rsqrt(spread + EPSILON) * norm_gain).astype(jnp.bfloat16)
    feature_count = model_width // narrow_count
    normed_share = lax.dynamic_slice_in_dim(normed, narrow_pos * feature_count, feature_count, 1)
    hidden_share = lax.dynamic_slice_in_dim(hidden, narrow_pos * feature_count, feature_count, 1)
    token_rows = expert_ids.shape[0]
    assign_count = token_rows * 2
    expert_count = w_gate_up.shape[0]
    unit_count = w_down.shape[1]
    flat_ids = expert_ids.reshape(assign_count)
    onehot = (flat_ids[:, None] == jnp.arange(expert_count, dtype=jnp.int32)[None, :]).astype(
        jnp.float32
    )
    strict_lower = (jnp.arange(assign_count)[:, None] > jnp.arange(assign_count)[None, :]).astype(
        jnp.float32
    )
    earlier = jnp.dot(strict_lower, onehot, precision=lax.Precision.HIGHEST)
    position = jnp.sum(earlier * onehot, axis=1).astype(jnp.int32)
    slot_pairs = (flat_ids * CAP + position).reshape(token_rows, 2)
    slot_range = jnp.arange(expert_count * CAP, dtype=jnp.int32)
    picks = slot_range[:, None, None] == slot_pairs[None, :, :]
    dispatch = jnp.any(picks, axis=2).astype(jnp.bfloat16)
    placed = jnp.dot(dispatch, normed_share, preferred_element_type=jnp.float32).astype(
        jnp.bfloat16
    )
    gathered = lax.all_gather(placed[None], "wide", axis=0, tiled=True)
    grouped = gathered.reshape(wide_count, expert_count, CAP, feature_count)
    gate_table = w_gate_up.reshape(expert_count, feature_count, 2 * unit_count)
    partial_sums = jnp.einsum(
        "wecd,edf->wecf", grouped, gate_table, preferred_element_type=jnp.float32
    )
    summed = lax.psum(partial_sums.astype(jnp.bfloat16), "narrow").astype(jnp.float32)
    hidden_all = activate(summed, unit_count)
    expert_rows = lax.psum_scatter(
        jnp.einsum("wecf,efd->wecd", hidden_all, w_down, preferred_element_type=jnp.float32).astype(
            jnp.bfloat16
        ),
        "wide",
        scatter_dimension=0,
        tiled=True,
    ).astype(jnp.float32)
    expert_flat = expert_rows.reshape(expert_count * CAP, feature_count)
    combine_table = jnp.sum(jnp.where(picks, route_weight[None, :, :], 0.0), axis=2)
    mixed = jnp.dot(jnp.transpose(combine_table), expert_flat, precision=lax.Precision.HIGHEST)
    return (hidden_share + mixed).astype(jnp.bfloat16)


def solution(mesh):
    return jax.shard_map(
        local,
        mesh=mesh,
        in_specs=(
            P("wide", None, None),
            P("wide", None, "narrow", None),
            P("wide", "narrow", None, None, None),
            P("wide", None),
            P("wide"),
            P("wide", None),
            P(),
            P("wide", None),
            P("wide", None),
            P(None, "narrow", None, "wide"),
            P(None, "wide", "narrow"),
        ),
        out_specs=P("wide", "narrow"),
        check_vma=False,
    )
```

profile of v0, /device:TPU:0, one launch (start us, length us, event | category | flops | bytes accessed | tf_op | source)
XLA Modules:
  0.0 793.6 jit_solution(6180339811328018294)
XLA Ops:
  6.5 0.9 select_reduce_fusion.1
  7.5 8.1 %fusion.45 = (bf16[2,4,1,128,2304]{4,3,2,1,0:T(8,128)(2,1)}, bf16[2,4,1,128,2304]{4,3,2,1,0:T(8,128)(2,1)}) fusion(bf16[2,4,2,128,2304]{4,3,2,1,0:T(8,128)(2,1)} %param.13), kind=kLoop, calls=%fused_computation.67 | loop fusion | bytes 18874368 | tf_op jit(solution)/shard_map/slice | solution.py:43
  15.6 8.4 %copy.63 = bf16[2,4,1,128,2304]{3,1,4,0,2:T(4,128)(2,1)} copy(bf16[2,4,1,128,2304]{4,3,2,1,0:T(8,128)(2,1)} %get-tuple-element.8) | data formatting | bytes 9437184 | tf_op jit(solution)/shard_map/slice | solution.py:42
  24.0 8.2 %reshape_squeeze.12 = bf16[2,512,36,64]{1,3,2,0:T(8,128)(2,1)} reshape(bf16[2,4,1,128,2304]{3,1,4,0,2:T(4,128)(2,1)} %copy.63) | data formatting | bytes 9437184 | tf_op jit(solution)/shard_map/reshape;squeeze | solution.py:42
  32.2 0.7 copy.62
  33.6 12.0 %fusion = (bf16[2,36,128]{2,1,0:T(8,128)(2,1)S(1)}, f32[2,36,128,512]{3,2,1,0:T(8,128)}) fusion(pred[2,512]{1,0:T(4,128)(4,1)S(1)} %fusion.37, bf16[2,128,36,64]{1,3,2,0:T(8,128)(2,1)S(1)} %bitcast.67, bf16[2,512,36,64]{1,3,2,0:T(8,128)(2,1)} %reshape_squeeze.12), kind=kOutput, calls=%fused_computation.2 | convolution fusion | flops 618126336 | bytes 24792064 | tf_op jit(solution)/shard_map/rqhd,rkhd->rhqk/dot_general | solution.py:56
  46.1 12.8 %pmax.7 = bf16[2,36,128]{2,1,0:T(8,128)(2,1)S(1)} all-reduce(bf16[2,36,128]{2,1,0:T(8,128)(2,1)S(1)} %max.7), channel_id=1, replica_groups=mesh['wide'=8,'narrow'=4] {'narrow'}, use_global_device_ids=true, to_apply=%region_3.4 | all-reduce | flops 9216 | bytes 36864 | tf_op jit(solution)/shard_map/pmax | solution.py:66
  59.0 8.3 %copy.65 = bf16[2,4,1,128,2304]{3,1,4,0,2:T(4,128)(2,1)} copy(bf16[2,4,1,128,2304]{4,3,2,1,0:T(8,128)(2,1)} %get-tuple-element.7) | data formatting | bytes 9437184 | tf_op jit(solution)/shard_map/slice | solution.py:43
  67.3 8.1 %reshape_squeeze.14 = bf16[2,512,36,64]{1,3,2,0:T(8,128)(2,1)} reshape(bf16[2,4,1,128,2304]{3,1,4,0,2:T(4,128)(2,1)} %copy.65) | data formatting | bytes 9437184 | tf_op jit(solution)/shard_map/reshape;squeeze | solution.py:43
  75.8 10.1 %fusion.8 = f32[2,36,128,64]{2,3,1,0:T(8,128)S(1)} fusion(bf16[2,512,36,64]{1,3,2,0:T(8,128)(2,1)} %reshape_squeeze.14, f32[2,36,128,512]{3,2,1,0:T(8,128)} %get-tuple-element.12, f32[2,36,128]{2,1,0:T(8,128)S(1)} %convert_element_type.70, pred[2,512]{1,0:T(4,128)(4,1)S(1)} %fusion.37), kind=kOutput, calls=%fused_computation.10 | convolution fusion | flops 627572736 | bytes 25990144 | tf_op jit(solution)/shard_map/rhqk,rkhd->rqhd/dot_general | solution.py:72
  85.9 0.6 fusion.20
  86.6 1.2 copy.67
  87.8 1.2 copy.92
  89.3 9.2 %fusion.4 = f32[2,36,128]{2,1,0:T(8,128)S(1)} fusion(f32[2,36,128,512]{3,2,1,0:T(8,128)} %get-tuple-element.12, f32[2,36,128]{2,1,0:T(8,128)S(1)} %convert_element_type.70, pred[2,512]{1,0:T(4,128)(4,1)S(1)} %fusion.37), kind=kLoop, calls=%fused_computation.8 | loop fusion | flops 23583744 | bytes 18949120 | tf_op jit(solution)/shard_map/reduce_sum | solution.py:71
  98.8 10.7 %psum.22 = bf16[2,128,36]{1,2,0:T(8,128)(2,1)S(1)} all-reduce(bf16[2,128,36]{1,2,0:T(8,128)(2,1)S(1)} %fusion.35), channel_id=1, replica_groups=mesh['wide'=8,'narrow'=4] {'narrow'}, use_global_device_ids=true, to_apply=%region_7.8 | all-reduce | flops 9216 | bytes 36864 | tf_op jit(solution)/shard_map/psum | solution.py:88
  109.6 0.6 copy.61
  111.0 0.8 dynamic-slice.2
  111.8 0.9 fusion.22
  112.7 14.2 %all-reduce.5.cloned.1.call-done = bf16[256,2304]{0,1:T(8,128)(2,1)} async-done(((bf16[256,2304]{0,1:T(8,128)(2,1)}), bf16[256,2304]{0,1:T(8,128)(2,1)}) %all-reduce.5.cloned.1.call-update) | async-done | bytes 1179664 | tf_op jit(solution)/shard_map/psum | solution.py:85
  127.5 1.9 multiply_reduce_fusion
  129.4 1.3 convolution_convert_fusion
  130.8 31.8 %reshape.120 = bf16[8,576,1440,1]{2,1,0,3:T(8,128)(2,1)} reshape(bf16[8,576,2,720]{3,2,1,0:T(2,128)(2,1)} %param.20) | data formatting | bytes 26542080 | tf_op jit(solution)/shard_map/reshape | solution.py:122
  162.7 62.8 %all-gather.3.cloned.1.call-done = bf16[5120,576]{0,1:T(8,128)(2,1)} async-done(((bf16[640,576]{0,1:T(8,128)(2,1)}), bf16[5120,576]{0,1:T(8,128)(2,1)}) %all-gather.3.cloned.1.call-update) | async-done | bytes 5898256 | tf_op jit(solution)/shard_map/all_gather | solution.py:120
  225.4 8.6 %copy.71 = bf16[5120,576]{1,0:T(8,128)(2,1)} copy(bf16[5120,576]{0,1:T(8,128)(2,1)} %all-gather.3.cloned.1.call-done) | data formatting | bytes 11796480 | tf_op jit(solution)/shard_map/all_gather | solution.py:120
  234.0 21.7 %convert_bitcast_fusion = bf16[8,8,80,1440]{3,2,0,1:T(8,128)(2,1)} fusion(bf16[8,576,1440,1]{2,1,0,3:T(8,128)(2,1)} %reshape.120, bf16[8,8,80,576]{3,2,1,0:T(8,128)(2,1)} %bitcast.70), kind=kOutput, calls=%fused_computation.5 | convolution fusion | flops 8500838400 | bytes 33914880 | tf_op jit(solution)/shard_map/wecd,edf->wecf/dot_general | solution.py:123
  256.0 269.5 %all-reduce.7.cloned.1.call-done = bf16[8,8,80,1440]{3,2,0,1:T(8,128)(2,1)} async-done(((bf16[8,8,80,1440]{3,2,0,1:T(8,128)(2,1)}), bf16[8,8,80,1440]{3,2,0,1:T(8,128)(2,1)}) %all-reduce.7.cloned.1.call-update) | async-done | bytes 14745616 | tf_op jit(solution)/shard_map/psum | solution.py:126
  525.5 18.0 %convert_element_type.83 = f32[8,8,80,1440]{3,2,0,1:T(8,128)} convert(bf16[8,8,80,1440]{3,2,0,1:T(8,128)(2,1)} %all-reduce.7.cloned.1.call-done) | non-fusion elementwise | flops 7372800 | bytes 44236800 | tf_op jit(solution)/shard_map/convert_element_type | solution.py:126
  543.5 19.3 %convert_bitcast_fusion.1 = bf16[8,8,80,576]{3,2,0,1:T(8,128)(2,1)} fusion(bf16[8,720,576]{1,2,0:T(8,128)(2,1)} %param.21, f32[8,8,80,1440]{3,2,0,1:T(8,128)} %convert_element_type.83), kind=kOutput, calls=%fused_computation.15 | convolution fusion | flops 4271800320 | bytes 42024960 | tf_op jit(solution)/shard_map/wecf,efd->wecd/dot_general | solution.py:129
  562.8 0.6 copy-done.7
  564.3 219.1 %all-reduce.9.cloned.1.call-done = bf16[8,8,80,576]{3,2,0,1:T(8,128)(2,1)} async-done(((bf16[8,8,80,576]{3,2,0,1:T(8,128)(2,1)}), bf16[8,8,80,576]{3,2,0,1:T(8,128)(2,1)}) %all-reduce.9.cloned.1.call-update) | async-done | bytes 5898256
  783.4 1.9 constant_dynamic-slice_fusion
  785.3 1.8 fusion.23
  (50 shorter events, 4.9 us)
Async XLA Ops:
  6.5 120.3 %all-reduce.5.cloned.1.call-start = ((), (), s32[]{:S(2)}) async-start(), calls=%async_computation | async-start | bytes 2359296 | tf_op jit(solution)/shard_map/psum | solution.py:85
  24.0 8.2 %copy-start = (bf16[2,128,2304]{2,1,0:T(8,128)(2,1)S(1)}, bf16[2,128,2304]{2,1,0:T(8,128)(2,1)}, u32[]{:S(2)}) copy-start(bf16[2,128,2304]{2,1,0:T(8,128)(2,1)} %param.11) | copy-start | bytes 3538948
  24.0 9.0 %copy-start.3 = (bf16[2,2,32,2304]{3,2,1,0:T(8,128)(2,1)S(1)}, bf16[2,2,32,2304]{3,2,1,0:T(8,128)(2,1)}, u32[]{:S(2)}) copy-start(bf16[2,2,32,2304]{3,2,1,0:T(8,128)(2,1)} %param.12) | copy-start | bytes 1769476
  24.0 9.5 %copy-start.6 = (s32[2]{0:T(128)S(1)}, s32[2]{0:T(128)}, u32[]{:S(2)}) copy-start(s32[2]{0:T(128)} %param.15) | copy-start | bytes 28
  89.0 20.5 %copy-start.1 = (bf16[256,2304]{1,0:T(8,128)(2,1)S(1)}, bf16[256,2304]{1,0:T(8,128)(2,1)}, u32[]{:S(2)}) copy-start(bf16[256,2304]{1,0:T(8,128)(2,1)} %param.16) | copy-start | bytes 3538948
  89.0 21.2 %copy-start.4 = (s32[256,2]{0,1:T(2,128)S(1)}, s32[256,2]{0,1:T(2,128)}, u32[]{:S(2)}) copy-start(s32[256,2]{0,1:T(2,128)} %param.18) | copy-start | bytes 6148
  89.0 136.4 %all-gather.3.cloned.1.call-start = ((), (), s32[]{:S(2)}) async-start(), calls=%async_computation.2 | async-start | bytes 6635520 | tf_op jit(solution)/shard_map/all_gather | solution.py:120
  126.9 2.6 copy-start.2
  130.8 394.7 %all-reduce.7.cloned.1.call-start = ((), (), s32[]{:S(2)}) async-start(), calls=%async_computation.1 | async-start | bytes 31457280 | tf_op jit(solution)/shard_map/psum | solution.py:126
  255.7 527.7 %all-reduce.9.cloned.1.call-start = ((), (), s32[]{:S(2)}) async-start(), calls=%async_computation.3 | async-start | bytes 13107200
  562.8 0.7 copy-start.7
  562.8 1.2 copy-start.5
Sparse Core Ops, SparseCore 0:
  89.1 37.6 all-reduce.4
  130.9 94.4 all-gather.2
  255.8 269.6 all-reduce.6
  562.9 220.4 all-reduce.8
where the time goes:
time: 796 us; the launch traced here: 794 us
  waiting for transfers between devices  566 us (71%)
  local copies, waits for them, and re-layouts  91.4 us (11%)
  matrix products  67.5 us (8%)
  other arithmetic  31.7 us (4%)
  blocking collectives  23.5 us (3%)
  between operations  13.3 us (2%)
    psum x1, waiting for transfers between devices, local(): lax.psum(partial_sums.astype(jnp.bfloat16), 'narrow').astype(jnp.float32)  270 us
    unnamed x5, waiting for transfers between devices  219 us
    all_gather x1, waiting for transfers between devices, local(): gathered = lax.all_gather(placed[None], 'wide', axis=0, tiled=True)  62.8 us
    reshape x1, local copies, waits for them, and re-layouts, local(): gate_table = w_gate_up.reshape(expert_count, feature_count, 2 * unit_count)  31.8 us
    dot_general x1, matrix products, local(): jnp.einsum('wecd,edf->wecf', grouped, gate_table, preferred_element_type=...  21.7 us
    dot_general x1, matrix products, local(): jnp.einsum('wecf,efd->wecd', hidden_all, w_down, preferred_element_type=j...  19.3 us
    convert_element_type x1, other arithmetic, local(): lax.psum(partial_sums.astype(jnp.bfloat16), 'narrow').astype(jnp.float32)  18 us
    slice x2, local copies, waits for them, and re-layouts, local(): cache_pool[:, :, 1].reshape(req_here, slot_count * page_len, head_count, HD)  16.5 us
  transfers between devices with their start and end apart: 4, of which 4 were waited for; matrix products, arithmetic and copies ran while one was open for 6% of the time, Pallas kernels for 0%

commit v1 on v0

v1 whole, which is shorter than its diff:
```python
import jax
import jax.numpy as jnp
from jax import lax
from jax.sharding import PartitionSpec as P

HD = 64
CAP = 80
CHUNKS = 4

NEG_FILL = -1e30
SCORE_SCALE = 0.125
EPSILON = 1e-05


def local(
    queries,
    new_kv,
    cache_pool,
    page_table,
    cached_len,
    residual,
    norm_gain,
    expert_ids,
    route_weight,
    w_gate_up,
    w_down,
):
    narrow_count = lax.axis_size("narrow")
    narrow_pos = lax.axis_index("narrow")
    wide_count = lax.axis_size("wide")
    req_here, new_len, model_width = queries.shape
    head_count = model_width // HD
    slot_count = cache_pool.shape[1]
    page_len = cache_pool.shape[3]
    local_new = new_kv.shape[2]
    table_len = page_table.shape[1]
    query_heads = queries.reshape(req_here, new_len, head_count, HD)
    cache_keys = cache_pool[:, :, 0].reshape(req_here, slot_count * page_len, head_count, HD)
    cache_vals = cache_pool[:, :, 1].reshape(req_here, slot_count * page_len, head_count, HD)
    new_keys = new_kv[:, 0].reshape(req_here, local_new, head_count, HD)
    new_vals = new_kv[:, 1].reshape(req_here, local_new, head_count, HD)
    own_slots = narrow_pos * slot_count + jnp.arange(slot_count, dtype=jnp.int32)
    matches = page_table[:, None, :] == own_slots[None, :, None]
    logical = jnp.sum(
        jnp.where(matches, jnp.arange(table_len, dtype=jnp.int32)[None, None, :], 0), axis=2
    )
    key_pos = logical[:, :, None] * page_len + jnp.arange(page_len, dtype=jnp.int32)[None, None, :]
    cache_valid = key_pos.reshape(req_here, slot_count * page_len) < cached_len[:, None]
    new_pos = narrow_pos * local_new + jnp.arange(local_new, dtype=jnp.int32)
    new_valid = new_pos[None, :] <= jnp.arange(new_len, dtype=jnp.int32)[:, None]
    cache_scores = (
        jnp.einsum("rqhd,rkhd->rhqk", query_heads, cache_keys, preferred_element_type=jnp.float32)
        * SCORE_SCALE
    )
    new_scores = (
        jnp.einsum("rqhd,rkhd->rhqk", query_heads, new_keys, preferred_element_type=jnp.float32)
        * SCORE_SCALE
    )
    cache_scores = jnp.where(cache_valid[:, None, None, :], cache_scores, NEG_FILL)
    new_scores = jnp.where(new_valid[None, None], new_scores, NEG_FILL)
    own_top = jnp.maximum(jnp.max(cache_scores, axis=3), jnp.max(new_scores, axis=3))
    cache_weights = jnp.where(
        cache_valid[:, None, None, :], jnp.exp(cache_scores - own_top[..., None]), 0.0
    )
    new_weights = jnp.where(new_valid[None, None], jnp.exp(new_scores - own_top[..., None]), 0.0)
    denominator = jnp.sum(cache_weights, axis=3) + jnp.sum(new_weights, axis=3)
    numerator = jnp.einsum(
        "rhqk,rkhd->rqhd",
        cache_weights.astype(jnp.bfloat16),
        cache_vals,
        preferred_element_type=jnp.float32,
    )
    numerator = numerator + jnp.einsum(
        "rhqk,rkhd->rqhd",
        new_weights.astype(jnp.bfloat16),
        new_vals,
        preferred_element_type=jnp.float32,
    )
    numerator = numerator.reshape(req_here * new_len, model_width).astype(jnp.bfloat16)
    stats = jnp.stack([own_top, denominator])
    stats = lax.all_gather(stats, "narrow", axis=0)
    feature_count = model_width // narrow_count
    token_rows = req_here * new_len
    pieces = numerator.reshape(token_rows, narrow_count, feature_count).transpose(1, 0, 2)
    pieces = lax.all_to_all(pieces, "narrow", 0, 0).astype(jnp.float32)
    tops, dens = stats[:, 0], stats[:, 1]
    factor = jnp.exp(tops - jnp.max(tops, axis=0, keepdims=True))
    factor = factor / jnp.sum(factor * dens, axis=0, keepdims=True)
    factor = factor.transpose(0, 1, 3, 2).reshape(narrow_count * token_rows, head_count)
    column_head = (narrow_pos * feature_count + jnp.arange(feature_count, dtype=jnp.int32)) // HD
    spread_heads = (
        jnp.arange(head_count, dtype=jnp.int32)[:, None] == column_head[None, :]
    ).astype(jnp.float32)
    factor = jnp.dot(factor, spread_heads, precision=lax.Precision.HIGHEST)
    attention = jnp.sum(pieces * factor.reshape(pieces.shape), axis=0)
    residual_share = lax.dynamic_slice_in_dim(residual, narrow_pos * feature_count, feature_count, 1)
    gain_share = lax.dynamic_slice_in_dim(norm_gain, narrow_pos * feature_count, feature_count, 0)
    hidden = residual_share.astype(jnp.float32) + attention
    squares = lax.all_gather(jnp.sum(hidden * hidden, axis=1), ("wide", "narrow"), axis=0)
    all_rows = lax.all_gather((hidden * gain_share).astype(jnp.bfloat16), "wide", axis=0)
    squares = jnp.sum(squares.reshape(wide_count, narrow_count, token_rows), axis=1)
    scale = lax.rsqrt(squares / model_width + EPSILON)
    normed = (all_rows.astype(jnp.float32) * scale[:, :, None]).astype(jnp.bfloat16)

    all_ids = lax.all_gather(expert_ids, "wide", axis=0)
    all_route = lax.all_gather(route_weight, "wide", axis=0)
    chips = narrow_count // 2
    chip, core = narrow_pos // 2, narrow_pos % 2
    block = wide_count // narrow_count
    far = jnp.arange(narrow_count, dtype=jnp.int32)
    owner = ((chip + far % chips) % chips) * 2 + (core + far // chips) % 2
    order = (owner[:, None] * block + jnp.arange(block, dtype=jnp.int32)[None, :]).reshape(-1)
    normed = normed[order]
    all_ids = all_ids[order]
    all_route = all_route[order]
    assign_count = token_rows * 2
    expert_count = w_gate_up.shape[0]
    flat_ids = all_ids.reshape(wide_count, assign_count)
    onehot = (
        flat_ids[:, :, None] == jnp.arange(expert_count, dtype=jnp.int32)[None, None, :]
    ).astype(jnp.bfloat16)
    strict_lower = (jnp.arange(assign_count)[:, None] > jnp.arange(assign_count)[None, :]).astype(
        jnp.bfloat16
    )
    earlier = jnp.einsum("ab,wbe->wae", strict_lower, onehot, preferred_element_type=jnp.float32)
    position = jnp.sum(earlier * onehot, axis=2).astype(jnp.int32)
    slot_pairs = (flat_ids * CAP + position).reshape(wide_count, token_rows, 2)
    slot_range = jnp.arange(expert_count * CAP, dtype=jnp.int32)
    picks = slot_range[None, :, None, None] == slot_pairs[:, None, :, :]
    dispatch = jnp.any(picks, axis=3).astype(jnp.bfloat16)
    combine_table = jnp.sum(jnp.where(picks, all_route[:, None, :, :], 0.0), axis=3)
    combine_table = combine_table.astype(jnp.bfloat16).reshape(
        wide_count, expert_count, CAP, token_rows
    )
    dispatch = dispatch.reshape(wide_count, expert_count, CAP, token_rows)
    placed = jnp.einsum(
        "wect,wtd->ewcd", dispatch, normed, preferred_element_type=jnp.float32
    ).astype(jnp.bfloat16)
    placed = placed.reshape(expert_count, wide_count * CAP, feature_count)

    core_pairs = [(n, n ^ 1) for n in range(narrow_count)]

    def chip_pairs(step):
        return [(n, (n + 2 * step) % narrow_count) for n in range(narrow_count)]

    table = jnp.transpose(w_gate_up, (2, 0, 1, 3))
    per_chunk = expert_count // CHUNKS
    rows_half = wide_count * CAP // 2
    rows_own = rows_half // chips
    out_chunks = []
    for chunk in range(CHUNKS):
        picked = slice(chunk * per_chunk, (chunk + 1) * per_chunk)
        partial = jnp.einsum(
            "erd,gedf->gerf", placed[picked], table[:, picked], preferred_element_type=jnp.float32
        ).astype(jnp.bfloat16)
        near = lax.ppermute(partial[:, :, rows_half:], "narrow", core_pairs)
        both = (
            partial[:, :, :rows_half].astype(jnp.float32) + near.astype(jnp.float32)
        )
        own = both[:, :, :rows_own]
        sent = both[:, :, rows_own:].astype(jnp.bfloat16)
        for step in range(1, chips):
            arrived = lax.ppermute(
                sent[:, :, (step - 1) * rows_own : step * rows_own], "narrow", chip_pairs(step)
            )
            own = own + arrived.astype(jnp.float32)
        active = (jax.nn.silu(own[0]) * own[1]).astype(jnp.bfloat16)
        mine = [active] + [
            lax.ppermute(active, "narrow", chip_pairs(chips - step)) for step in range(1, chips)
        ]
        mine = jnp.concatenate(mine, axis=1)
        other = lax.ppermute(mine, "narrow", core_pairs)
        whole = jnp.concatenate([mine, other], axis=1)
        out_chunks.append(
            jnp.einsum(
                "erf,efd->erd", whole, w_down[picked], preferred_element_type=jnp.float32
            ).astype(jnp.bfloat16)
        )
    outs = jnp.concatenate(out_chunks, axis=0).reshape(
        expert_count, wide_count, CAP, feature_count
    )
    mixed = jnp.einsum(
        "wect,ewcd->wtd", combine_table, outs, preferred_element_type=jnp.float32
    ).astype(jnp.bfloat16)
    back = jnp.argsort(order)
    mixed = lax.all_to_all(mixed[back], "wide", 0, 0)
    mixed = jnp.sum(mixed.astype(jnp.float32), axis=0)
    return (hidden + mixed).astype(jnp.bfloat16)


def solution(mesh):
    return jax.shard_map(
        local,
        mesh=mesh,
        in_specs=(
            P("wide", None, None),
            P("wide", None, "narrow", None),
            P("wide", "narrow", None, None, None),
            P("wide", None),
            P("wide"),
            P("wide", None),
            P(),
            P("wide", None),
            P("wide", None),
            P(None, "narrow", None, "wide"),
            P(None, "wide", "narrow"),
        ),
        out_specs=P("wide", "narrow"),
        check_vma=False,
    )
```

time: 796 us -> 524 us (0.66)
  waiting for transfers between devices: 566 us -> 104 us
  blocking collectives: 23.5 us -> 157 us
  local copies, waits for them, and re-layouts: 91.4 us -> 116 us
  other arithmetic: 31.7 us -> 48.8 us
  starting transfers between devices: 0.53 us -> 10.7 us
    psum x2 -> x0, waiting for transfers between devices: 284 us -> none  [the longest x1 270 us: local(): lax.psum(partial_sums.astype(jnp.bfloat16), 'narrow').astype(jnp.float32)]
    unnamed x5 -> x1, waiting for transfers between devices: 219 us -> 0.02 us
    ppermute x0 -> x16, waiting for transfers between devices: none -> 104 us  [the longest x4 75.4 us: local(): lax.ppermute(sent[:, :, (step - 1) * rows_own:step * rows_own], 'narrow',...]
    all_gather x0 -> x4, blocking collectives: none -> 100 us  [the longest x1 39.2 us: local(): lax.all_gather(jnp.sum(hidden * hidden, axis=1), ('wide', 'narrow'), axis=0)]
    all_gather x1, waiting for transfers between devices: 62.8 us -> 0.02 us  [local(): lax.all_gather((hidden * gain_share).astype(jnp.bfloat16), 'wide', axis=0)]
    all_to_all x0 -> x1, blocking collectives: none -> 56.8 us  [local(): mixed = lax.all_to_all(mixed[back], 'wide', 0, 0)]
    reshape x1, local copies, waits for them, and re-layouts: 31.8 us -> 0.01 us  [local(): squares.reshape(wide_count, narrow_count, token_rows)]
    unnamed x23 -> x76, local copies, waits for them, and re-layouts: 5.85 us -> 22.1 us
  transfers between devices with their start and end apart: 4 -> 18, of which waited for: 4 -> 7; matrix products, arithmetic and copies ran while one was open for 6% -> 19% of each run, Pallas kernels for 0% -> 0%
where the time goes in v1:
time: 524 us; the launch traced here: 515 us
  blocking collectives  157 us (30%)
  local copies, waits for them, and re-layouts  116 us (22%)
  waiting for transfers between devices  104 us (20%)
  matrix products  64.2 us (12%)
  other arithmetic  48.8 us (9%)
  between operations  14.7 us (3%)
  starting transfers between devices  10.7 us (2%)
    ppermute x4, waiting for transfers between devices, local(): lax.ppermute(sent[:, :, (step - 1) * rows_own:step * rows_own], 'narrow',...  75.4 us
    all_to_all x1, blocking collectives, local(): mixed = lax.all_to_all(mixed[back], 'wide', 0, 0)  56.8 us
    all_gather x1, blocking collectives, local(): lax.all_gather(jnp.sum(hidden * hidden, axis=1), ('wide', 'narrow'), axis=0)  39.2 us
    ppermute x4, waiting for transfers between devices, local(): lax.ppermute(active, 'narrow', chip_pairs(chips - step))  28.7 us
    all_gather x1, blocking collectives, local(): all_ids = lax.all_gather(expert_ids, 'wide', axis=0)  27.2 us
    all_gather x1, blocking collectives, local(): all_route = lax.all_gather(route_weight, 'wide', axis=0)  26.2 us
    unnamed x76, local copies, waits for them, and re-layouts  22.1 us
    slice x2, local copies, waits for them, and re-layouts, local(): cache_pool[:, :, 0].reshape(req_here, slot_count * page_len, head_count, HD)  16.5 us
  transfers between devices with their start and end apart: 18, of which 7 were waited for; matrix products, arithmetic and copies ran while one was open for 19% of the time, Pallas kernels for 0%

profile of v1, /device:TPU:0, one launch (start us, length us, event | category | flops | bytes accessed | tf_op | source)
XLA Modules:
  0.0 515.1 jit_solution(14048328369082441519)
XLA Ops:
  7.6 8.2 %fusion.131 = (bf16[2,4,1,128,2304]{4,3,2,1,0:T(8,128)(2,1)}, bf16[2,4,1,128,2304]{4,3,2,1,0:T(8,128)(2,1)}) fusion(bf16[2,4,2,128,2304]{4,3,2,1,0:T(8,128)(2,1)} %param.13), kind=kLoop, calls=%fused_computation.192 | loop fusion | bytes 18874368 | tf_op jit(solution)/shard_map/slice | solution.py:38
  15.8 8.3 %copy.263 = bf16[2,4,1,128,2304]{3,1,4,0,2:T(4,128)(2,1)} copy(bf16[2,4,1,128,2304]{4,3,2,1,0:T(8,128)(2,1)} %get-tuple-element.11) | data formatting | bytes 9437184 | tf_op jit(solution)/shard_map/slice | solution.py:38
  24.1 8.1 %reshape_squeeze.12 = bf16[2,512,36,64]{1,3,2,0:T(8,128)(2,1)} reshape(bf16[2,4,1,128,2304]{3,1,4,0,2:T(4,128)(2,1)} %copy.263) | data formatting | bytes 9437184 | tf_op jit(solution)/shard_map/reshape;squeeze | solution.py:38
  35.5 8.4 %copy.265 = bf16[2,4,1,128,2304]{3,1,4,0,2:T(4,128)(2,1)} copy(bf16[2,4,1,128,2304]{4,3,2,1,0:T(8,128)(2,1)} %get-tuple-element.12) | data formatting | bytes 9437184 | tf_op jit(solution)/shard_map/slice | solution.py:39
  43.8 8.1 %reshape_squeeze.14 = bf16[2,512,36,64]{1,3,2,0:T(8,128)(2,1)} reshape(bf16[2,4,1,128,2304]{3,1,4,0,2:T(4,128)(2,1)} %copy.265) | data formatting | bytes 9437184 | tf_op jit(solution)/shard_map/reshape;squeeze | solution.py:39
  53.3 12.2 %fusion.1 = (f32[2,36,128]{2,1,0:T(8,128)S(1)}, f32[2,36,128,512]{3,2,1,0:T(8,128)}) fusion(pred[2,512]{1,0:T(4,128)(4,1)S(1)} %fusion.111, bf16[2,128,36,64]{1,3,2,0:T(8,128)(2,1)S(1)} %bitcast.150, bf16[2,512,36,64]{1,3,2,0:T(8,128)(2,1)} %reshape_squeeze.12), kind=kOutput, calls=%fused_computation.7 | convolution fusion | flops 618126336 | bytes 24810496 | tf_op jit(solution)/shard_map/rqhd,rkhd->rhqk/dot_general | solution.py:52
  65.9 9.0 %fusion.5 = f32[2,36,128,64]{2,3,1,0:T(8,128)S(1)} fusion(bf16[2,512,36,64]{1,3,2,0:T(8,128)(2,1)S(1)} %copy-done.4, f32[2,36,128,512]{3,2,1,0:T(8,128)} %get-tuple-element.24, f32[2,36,128]{2,1,0:T(8,128)S(1)} %max.17, pred[2,512]{1,0:T(4,128)(4,1)S(1)} %fusion.111), kind=kOutput, calls=%fused_computation.14 | convolution fusion | flops 627572736 | bytes 25990144 | tf_op jit(solution)/shard_map/rhqk,rkhd->rqhd/dot_general | solution.py:67
  78.5 4.2 all-to-all-start
  83.2 10.0 %fusion.2 = f32[2,36,128]{2,1,0:T(8,128)S(1)} fusion(f32[2,36,128,512]{3,2,1,0:T(8,128)} %get-tuple-element.24, f32[2,36,128]{2,1,0:T(8,128)} %copy-done.26, pred[2,512]{1,0:T(4,128)(4,1)S(1)} %fusion.111), kind=kLoop, calls=%fused_computation.9 | loop fusion | flops 23583744 | bytes 18949120 | tf_op jit(solution)/shard_map/reduce_sum | solution.py:66
  93.6 7.4 %all-gather = f32[8,2,36,128]{3,1,2,0:T(2,128)S(1)} all-gather(f32[2,2,36,128]{3,1,2,0:T(2,128)S(1)} %pad_maximum_fusion.5), channel_id=2, replica_groups=mesh['wide'=8,'narrow'=4] {'narrow'}, dimensions={0}, use_global_device_ids=true | all-gather | bytes 368640 | tf_op jit(solution)/shard_map/all_gather | solution.py:81
  105.3 27.2 %all-gather.1 = s32[2048,2]{0,1:T(2,128)S(1)} all-gather(s32[256,2]{0,1:T(2,128)S(1)} %copy-done.33), channel_id=3, replica_groups=mesh['wide'=8,'narrow'=4] {'wide'}, dimensions={0}, use_global_device_ids=true | all-gather | bytes 18432 | tf_op jit(solution)/shard_map/all_gather | solution.py:105
  134.0 8.8 %copy.367 = bf16[8,576,2,720]{3,1,2,0:T(8,128)(2,1)S(1)} copy(bf16[8,576,2,720]{3,2,1,0:T(2,128)(2,1)} %param.20) | data formatting | bytes 26542080 | tf_op args[9]
  142.8 7.2 %fusion.4 = pred[8,640,256]{2,1,0:T(8,128)(4,1)} fusion(s32[8,256,2]{1,2,0:T(2,128)S(1)} %copy.279), kind=kLoop, calls=%fused_computation.13 | loop fusion | flops 3932160 | bytes 1327104 | tf_op jit(solution)/shard_map/reduce_or | solution.py:130
  149.9 5.2 %fusion.130 = (bf16[2,2,576,720]{3,2,0,1:T(8,128)(2,1)}, bf16[2,2,576,720]{3,2,0,1:T(8,128)(2,1)}, bf16[2,2,576,720]{3,2,0,1:T(8,128)(2,1)}, bf16[2,2,576,720]{3,2,0,1:T(8,128)(2,1)}) fusion(bf16[2,8,576,720]{3,2,0,1:T(8,128)(2,1)S(1)} %bitcast.148), kind=kLoop, calls=%fused_computation.191 | loop fusion | bytes 26542080 | tf_op jit(solution)/shard_map/slice | solution.py:154
  155.1 39.2 %all-gather.5 = f32[32,1,256]{2,1,0:T(1,128)S(1)} all-gather(f32[1,1,256]{2,1,0:T(1,128)S(1)} %bitcast.165), channel_id=6, replica_groups=mesh['wide'=8,'narrow'=4] {'wide','narrow'}, dimensions={0}, use_global_device_ids=true | all-gather | bytes 33792 | tf_op jit(solution)/shard_map/all_gather | solution.py:99
  201.0 3.6 convert_bitcast_fusion
  214.1 3.5 convert_bitcast_fusion.3
  228.6 3.5 convert_bitcast_fusion.1
  235.8 26.2 %all-gather.2 = f32[2048,2]{0,1:T(2,128)S(1)} all-gather(f32[256,2]{0,1:T(2,128)S(1)} %copy-done.34), channel_id=4, replica_groups=mesh['wide'=8,'narrow'=4] {'wide'}, dimensions={0}, use_global_device_ids=true | all-gather | bytes 18432 | tf_op jit(solution)/shard_map/all_gather | solution.py:106
  277.2 14.0 %collective-permute-done.1 = bf16[2,2,160,720]{3,2,1,0:T(8,128)(2,1)S(1)} collective-permute-done((bf16[2,2,160,720]{3,2,1,0:T(8,128)(2,1)S(1)}, bf16[2,2,160,720]{3,2,1,0:T(8,128)(2,1)S(1)}, u32[]{:S(2)}, u32[]{:S(2)}) %collective-permute-start.1) | collective-permute-done | bytes 921632 | tf_op jit(solution)/shard_map/ppermute | solution.py:163
  291.8 20.5 %collective-permute-done.5 = bf16[2,2,160,720]{3,2,1,0:T(8,128)(2,1)S(1)} collective-permute-done((bf16[2,2,160,720]{3,2,1,0:T(8,128)(2,1)S(1)}, bf16[2,2,160,720]{3,2,1,0:T(8,128)(2,1)S(1)}, u32[]{:S(2)}, u32[]{:S(2)}) %collective-permute-start.5) | collective-permute-done | bytes 921632 | tf_op jit(solution)/shard_map/ppermute | solution.py:163
  312.8 20.5 %collective-permute-done.9 = bf16[2,2,160,720]{3,2,1,0:T(8,128)(2,1)S(1)} collective-permute-done((bf16[2,2,160,720]{3,2,1,0:T(8,128)(2,1)S(1)}, bf16[2,2,160,720]{3,2,1,0:T(8,128)(2,1)S(1)}, u32[]{:S(2)}, u32[]{:S(2)}) %collective-permute-start.9) | collective-permute-done | bytes 921632 | tf_op jit(solution)/shard_map/ppermute | solution.py:163
  333.9 20.5 %collective-permute-done.13 = bf16[2,2,160,720]{3,2,1,0:T(8,128)(2,1)S(1)} collective-permute-done((bf16[2,2,160,720]{3,2,1,0:T(8,128)(2,1)S(1)}, bf16[2,2,160,720]{3,2,1,0:T(8,128)(2,1)S(1)}, u32[]{:S(2)}, u32[]{:S(2)}) %collective-permute-start.13) | collective-permute-done | bytes 921632 | tf_op jit(solution)/shard_map/ppermute | solution.py:163
  354.6 10.3 %collective-permute-done.2 = bf16[2,160,720]{2,1,0:T(8,128)(2,1)S(1)} collective-permute-done((bf16[2,160,720]{2,1,0:T(8,128)(2,1)S(1)}, bf16[2,160,720]{2,1,0:T(8,128)(2,1)S(1)}, u32[]{:S(2)}, u32[]{:S(2)}) %collective-permute-start.2) | collective-permute-done | bytes 460832 | tf_op jit(solution)/shard_map/ppermute | solution.py:169
  366.3 9.1 %collective-permute-done.6 = bf16[2,160,720]{2,1,0:T(8,128)(2,1)S(1)} collective-permute-done((bf16[2,160,720]{2,1,0:T(8,128)(2,1)S(1)}, bf16[2,160,720]{2,1,0:T(8,128)(2,1)S(1)}, u32[]{:S(2)}, u32[]{:S(2)}) %collective-permute-start.6) | collective-permute-done | bytes 460832 | tf_op jit(solution)/shard_map/ppermute | solution.py:169
  376.5 9.3 %collective-permute-done.10 = bf16[2,160,720]{2,1,0:T(8,128)(2,1)S(1)} collective-permute-done((bf16[2,160,720]{2,1,0:T(8,128)(2,1)S(1)}, bf16[2,160,720]{2,1,0:T(8,128)(2,1)S(1)}, u32[]{:S(2)}, u32[]{:S(2)}) %collective-permute-start.10) | collective-permute-done | bytes 460832 | tf_op jit(solution)/shard_map/ppermute | solution.py:169
  413.3 4.6 fusion.68
  418.0 4.4 fusion.63
  424.0 3.5 fusion.58
  430.7 8.6 %copy.306 = bf16[8,640,576]{2,1,0:T(8,128)(2,1)} copy(bf16[8,640,576]{1,2,0:T(8,128)(2,1)} %pad_maximum_fusion) | data formatting | bytes 11796480 | tf_op jit(solution)/shard_map/concatenate | solution.py:179
  439.3 7.4 %bitcast_convert_fusion = bf16[8,256,576]{1,2,0:T(8,128)(2,1)} fusion(bf16[8,8,80,256]{3,2,1,0:T(8,128)(2,1)} %bitcast.154, bf16[8,8,80,576]{3,2,1,0:T(8,128)(2,1)} %bitcast.152), kind=kOutput, calls=%fused_computation.22 | convolution fusion | flops 1511129088 | bytes 10878976 | tf_op jit(solution)/shard_map/wect,ewcd->wtd/dot_general | solution.py:182
  449.0 56.8 %all_to_all.10 = bf16[8,256,576]{1,2,0:T(8,128)(2,1)S(1)} all-to-all(bf16[8,256,576]{1,2,0:T(8,128)(2,1)S(1)} %gather_fusion.3), channel_id=1, replica_groups=mesh['wide'=8,'narrow'=4] {'wide'}, dimensions={0} | all-to-all | bytes 4718592 | tf_op jit(solution)/shard_map/all_to_all | solution.py:186
  (210 shorter events, 102.9 us)
Async XLA Ops:
  6.5 95.2 %copy-start = (bf16[256,2304]{1,0:T(8,128)(2,1)S(1)}, bf16[256,2304]{1,0:T(8,128)(2,1)}, u32[]{:S(2)}) copy-start(bf16[256,2304]{1,0:T(8,128)(2,1)} %param.16) | copy-start | bytes 3538948
  24.1 8.1 %copy-start.24 = (bf16[2,128,2304]{2,1,0:T(8,128)(2,1)S(1)}, bf16[2,128,2304]{2,1,0:T(8,128)(2,1)}, u32[]{:S(2)}) copy-start(bf16[2,128,2304]{2,1,0:T(8,128)(2,1)} %param.11) | copy-start | bytes 3538948
  43.8 9.4 %copy-start.35 = (s32[2]{0:T(128)S(1)}, s32[2]{0:T(128)}, u32[]{:S(2)}) copy-start(s32[2]{0:T(128)} %param.15) | copy-start | bytes 28
  53.3 12.2 %copy-start.19 = (bf16[2,32,36,64]{3,2,1,0:T(8,128)(2,1)S(1)}, bf16[2,32,36,64]{3,2,1,0:T(8,128)(2,1)}, u32[]{:S(2)}) copy-start(bf16[2,32,36,64]{3,2,1,0:T(8,128)(2,1)} %reshape_squeeze.13) | copy-start | bytes 884740
  53.3 12.7 %copy-start.4 = (bf16[2,512,36,64]{1,3,2,0:T(8,128)(2,1)S(1)}, bf16[2,512,36,64]{1,3,2,0:T(8,128)(2,1)}, u32[]{:S(2)}) copy-start(bf16[2,512,36,64]{1,3,2,0:T(8,128)(2,1)} %reshape_squeeze.14) | copy-start | bytes 14155780
  65.9 9.1 %copy-start.26 = (f32[2,36,128]{2,1,0:T(8,128)}, f32[2,36,128]{2,1,0:T(8,128)S(1)}, u32[]{:S(2)}) copy-start(f32[2,36,128]{2,1,0:T(8,128)S(1)} %max.17) | copy-start | bytes 110596
  65.9 9.1 %copy-start.18 = (bf16[2,32,36,64]{3,2,1,0:T(8,128)(2,1)S(1)}, bf16[2,32,36,64]{3,2,1,0:T(8,128)(2,1)}, u32[]{:S(2)}) copy-start(bf16[2,32,36,64]{3,2,1,0:T(8,128)(2,1)} %reshape_squeeze.15) | copy-start | bytes 884740
  78.5 24.5 %all-to-all-start = ((bf16[4,256,576]{1,2,0:T(8,128)(2,1)}), bf16[4,256,576]{1,2,0:T(8,128)(2,1)S(1)}, u32[]{:S(2)}, u32[]{:S(2)}) async-start(bf16[4,256,576]{1,2,0:T(8,128)(2,1)} %bitcast.3), calls=%async_computation | async-start | bytes 2359296 | tf_op jit(solution)/shard_map/all_to_all | solution.py:85
  82.7 111.9 %all-gather.8.cloned.1.call-start = ((), (), s32[]{:S(2)}) async-start(), calls=%async_computation.2 | async-start | bytes 2654208 | tf_op jit(solution)/shard_map/all_gather | solution.py:100
  83.1 10.0 %copy-start.27 = (f32[2,36,128]{2,1,0:T(8,128)S(1)}, f32[2,36,128]{2,1,0:T(8,128)}, u32[]{:S(2)}) copy-start(f32[2,36,128]{2,1,0:T(8,128)} %copy-done.26) | copy-start | bytes 110596
  102.1 31.0 %copy-start.16 = (bf16[256,576]{0,1:T(8,128)(2,1)}, bf16[256,576]{0,1:T(8,128)(2,1)S(1)}, u32[]{:S(2)}) copy-start(bf16[256,576]{0,1:T(8,128)(2,1)S(1)} %copy.329) | copy-start | bytes 884740
  211.4 52.2 %collective-permute-start = (bf16[2,2,320,720]{3,2,1,0:T(8,128)(2,1)}, bf16[2,2,320,720]{3,2,1,0:T(8,128)(2,1)}, u32[]{:S(2)}, u32[]{:S(2)}) collective-permute-start(bf16[2,2,320,720]{3,2,1,0:T(8,128)(2,1)} %slice.201), channel_id=1, source_target_pairs={{0,1},{1,0},{2,3},{3,2},{4,5},{5,4},{6,7},{7,6},{8,9},{9,8},{10,11... | collective-permute-start | bytes 5529608 | tf_op jit(solution)/shard_map/ppermute | solution.py:156
  219.0 47.4 %collective-permute-start.4 = (bf16[2,2,320,720]{3,2,1,0:T(8,128)(2,1)}, bf16[2,2,320,720]{3,2,1,0:T(8,128)(2,1)}, u32[]{:S(2)}, u32[]{:S(2)}) collective-permute-start(bf16[2,2,320,720]{3,2,1,0:T(8,128)(2,1)} %slice.209), channel_id=1, source_target_pairs={{0,1},{1,0},{2,3},{3,2},{4,5},{5,4},{6,7},{7,6},{8,9},{9,8},{10,11... | collective-permute-start | bytes 5529608 | tf_op jit(solution)/shard_map/ppermute | solution.py:156
  225.3 45.5 %collective-permute-start.8 = (bf16[2,2,320,720]{3,2,1,0:T(8,128)(2,1)S(1)}, bf16[2,2,320,720]{3,2,1,0:T(8,128)(2,1)}, u32[]{:S(2)}, u32[]{:S(2)}) collective-permute-start(bf16[2,2,320,720]{3,2,1,0:T(8,128)(2,1)S(1)} %slice.217), channel_id=1, source_target_pairs={{0,1},{1,0},{2,3},{3,2},{4,5},{5,4},{6,7},{7,6},{8,9},{9,8},{10,11... | collective-permute-start | bytes 5529608 | tf_op jit(solution)/shard_map/ppermute | solution.py:156
  235.4 38.1 %collective-permute-start.12 = (bf16[2,2,320,720]{3,2,1,0:T(8,128)(2,1)}, bf16[2,2,320,720]{3,2,1,0:T(8,128)(2,1)}, u32[]{:S(2)}, u32[]{:S(2)}) collective-permute-start(bf16[2,2,320,720]{3,2,1,0:T(8,128)(2,1)} %slice.225), channel_id=1, source_target_pairs={{0,1},{1,0},{2,3},{3,2},{4,5},{5,4},{6,7},{7,6},{8,9},{9,8},{10,11... | collective-permute-start | bytes 5529608 | tf_op jit(solution)/shard_map/ppermute | solution.py:156
  266.4 24.8 %collective-permute-start.1 = (bf16[2,2,160,720]{3,2,1,0:T(8,128)(2,1)S(1)}, bf16[2,2,160,720]{3,2,1,0:T(8,128)(2,1)S(1)}, u32[]{:S(2)}, u32[]{:S(2)}) collective-permute-start(bf16[2,2,160,720]{3,2,1,0:T(8,128)(2,1)S(1)} %slice.293), channel_id=1, source_target_pairs={{0,2},{1,3},{2,0},{3,1},{4,6},{5,7},{6,4},{7,5},{8,10},{9,11},{10,... | collective-permute-start | bytes 2764808 | tf_op jit(solution)/shard_map/ppermute | solution.py:163
  269.0 43.2 %collective-permute-start.5 = (bf16[2,2,160,720]{3,2,1,0:T(8,128)(2,1)S(1)}, bf16[2,2,160,720]{3,2,1,0:T(8,128)(2,1)S(1)}, u32[]{:S(2)}, u32[]{:S(2)}) collective-permute-start(bf16[2,2,160,720]{3,2,1,0:T(8,128)(2,1)S(1)} %slice.292), channel_id=1, source_target_pairs={{0,2},{1,3},{2,0},{3,1},{4,6},{5,7},{6,4},{7,5},{8,10},{9,11},{10,... | collective-permute-start | bytes 2764808 | tf_op jit(solution)/shard_map/ppermute | solution.py:163
  273.0 60.3 %collective-permute-start.9 = (bf16[2,2,160,720]{3,2,1,0:T(8,128)(2,1)S(1)}, bf16[2,2,160,720]{3,2,1,0:T(8,128)(2,1)S(1)}, u32[]{:S(2)}, u32[]{:S(2)}) collective-permute-start(bf16[2,2,160,720]{3,2,1,0:T(8,128)(2,1)S(1)} %slice.291), channel_id=1, source_target_pairs={{0,2},{1,3},{2,0},{3,1},{4,6},{5,7},{6,4},{7,5},{8,10},{9,11},{10,... | collective-permute-start | bytes 2764808 | tf_op jit(solution)/shard_map/ppermute | solution.py:163
  275.5 78.8 %collective-permute-start.13 = (bf16[2,2,160,720]{3,2,1,0:T(8,128)(2,1)S(1)}, bf16[2,2,160,720]{3,2,1,0:T(8,128)(2,1)S(1)}, u32[]{:S(2)}, u32[]{:S(2)}) collective-permute-start(bf16[2,2,160,720]{3,2,1,0:T(8,128)(2,1)S(1)} %slice.290), channel_id=1, source_target_pairs={{0,2},{1,3},{2,0},{3,1},{4,6},{5,7},{6,4},{7,5},{8,10},{9,11},{10,... | collective-permute-start | bytes 2764808 | tf_op jit(solution)/shard_map/ppermute | solution.py:163
  291.7 73.2 %collective-permute-start.2 = (bf16[2,160,720]{2,1,0:T(8,128)(2,1)S(1)}, bf16[2,160,720]{2,1,0:T(8,128)(2,1)S(1)}, u32[]{:S(2)}, u32[]{:S(2)}) collective-permute-start(bf16[2,160,720]{2,1,0:T(8,128)(2,1)S(1)} %fusion.93), channel_id=1, source_target_pairs={{0,2},{1,3},{2,0},{3,1},{4,6},{5,7},{6,4},{7,5},{8,10},{9,11},{10,... | collective-permute-start | bytes 1382408 | tf_op jit(solution)/shard_map/ppermute | solution.py:169
  312.7 62.7 %collective-permute-start.6 = (bf16[2,160,720]{2,1,0:T(8,128)(2,1)S(1)}, bf16[2,160,720]{2,1,0:T(8,128)(2,1)S(1)}, u32[]{:S(2)}, u32[]{:S(2)}) collective-permute-start(bf16[2,160,720]{2,1,0:T(8,128)(2,1)S(1)} %fusion.91), channel_id=1, source_target_pairs={{0,2},{1,3},{2,0},{3,1},{4,6},{5,7},{6,4},{7,5},{8,10},{9,11},{10,... | collective-permute-start | bytes 1382408 | tf_op jit(solution)/shard_map/ppermute | solution.py:169
  333.8 52.0 %collective-permute-start.10 = (bf16[2,160,720]{2,1,0:T(8,128)(2,1)S(1)}, bf16[2,160,720]{2,1,0:T(8,128)(2,1)S(1)}, u32[]{:S(2)}, u32[]{:S(2)}) collective-permute-start(bf16[2,160,720]{2,1,0:T(8,128)(2,1)S(1)} %fusion.89), channel_id=1, source_target_pairs={{0,2},{1,3},{2,0},{3,1},{4,6},{5,7},{6,4},{7,5},{8,10},{9,11},{10,... | collective-permute-start | bytes 1382408 | tf_op jit(solution)/shard_map/ppermute | solution.py:169
  365.9 38.1 %collective-permute-start.3 = (bf16[2,320,720]{2,1,0:T(8,128)(2,1)}, bf16[2,320,720]{2,1,0:T(8,128)(2,1)}, u32[]{:S(2)}, u32[]{:S(2)}) collective-permute-start(bf16[2,320,720]{2,1,0:T(8,128)(2,1)} %pad_maximum_fusion.1), channel_id=1, source_target_pairs={{0,1},{1,0},{2,3},{3,2},{4,5},{5,4},{6,7},{7,6},{8,9},{9,8},{10,11... | collective-permute-start | bytes 2764808 | tf_op jit(solution)/shard_map/ppermute | solution.py:172
  366.2 29.5 %collective-permute-start.14 = (bf16[2,160,720]{2,1,0:T(8,128)(2,1)S(1)}, bf16[2,160,720]{2,1,0:T(8,128)(2,1)}, u32[]{:S(2)}, u32[]{:S(2)}) collective-permute-start(bf16[2,160,720]{2,1,0:T(8,128)(2,1)S(1)} %fusion.87), channel_id=1, source_target_pairs={{0,2},{1,3},{2,0},{3,1},{4,6},{5,7},{6,4},{7,5},{8,10},{9,11},{10,... | collective-permute-start | bytes 1382408 | tf_op jit(solution)/shard_map/ppermute | solution.py:169
  376.5 32.8 %collective-permute-start.7 = (bf16[2,320,720]{2,1,0:T(8,128)(2,1)}, bf16[2,320,720]{2,1,0:T(8,128)(2,1)}, u32[]{:S(2)}, u32[]{:S(2)}) collective-permute-start(bf16[2,320,720]{2,1,0:T(8,128)(2,1)} %pad_maximum_fusion.2), channel_id=1, source_target_pairs={{0,1},{1,0},{2,3},{3,2},{4,5},{5,4},{6,7},{7,6},{8,9},{9,8},{10,11... | collective-permute-start | bytes 2764808 | tf_op jit(solution)/shard_map/ppermute | solution.py:172
  387.6 23.4 %collective-permute-start.11 = (bf16[2,320,720]{2,1,0:T(8,128)(2,1)}, bf16[2,320,720]{2,1,0:T(8,128)(2,1)}, u32[]{:S(2)}, u32[]{:S(2)}) collective-permute-start(bf16[2,320,720]{2,1,0:T(8,128)(2,1)} %pad_maximum_fusion.3), channel_id=1, source_target_pairs={{0,1},{1,0},{2,3},{3,2},{4,5},{5,4},{6,7},{7,6},{8,9},{9,8},{10,11... | collective-permute-start | bytes 2764808 | tf_op jit(solution)/shard_map/ppermute | solution.py:172
  395.7 5.0 copy-start.21
  397.9 24.4 %collective-permute-start.15 = (bf16[2,320,720]{2,1,0:T(8,128)(2,1)}, bf16[2,320,720]{2,1,0:T(8,128)(2,1)}, u32[]{:S(2)}, u32[]{:S(2)}) collective-permute-start(bf16[2,320,720]{2,1,0:T(8,128)(2,1)} %pad_maximum_fusion.4), channel_id=1, source_target_pairs={{0,1},{1,0},{2,3},{3,2},{4,5},{5,4},{6,7},{7,6},{8,9},{9,8},{10,11... | collective-permute-start | bytes 2764808 | tf_op jit(solution)/shard_map/ppermute | solution.py:172
  400.7 5.2 %copy-start.32 = (bf16[2,160,720]{1,2,0:T(8,128)(2,1)S(1)}, bf16[2,160,720]{1,2,0:T(8,128)(2,1)}, u32[]{:S(2)}) copy-start(bf16[2,160,720]{1,2,0:T(8,128)(2,1)} %copy.285) | copy-start | bytes 1382404
  413.3 4.6 copy-start.29
  418.0 6.0 %copy-start.28 = (bf16[2,160,720]{1,2,0:T(8,128)(2,1)S(1)}, bf16[2,160,720]{1,2,0:T(8,128)(2,1)}, u32[]{:S(2)}) copy-start(bf16[2,160,720]{1,2,0:T(8,128)(2,1)} %copy.303) | copy-start | bytes 1382404
  449.0 58.8 %copy-start.1 = (bf16[256,2304]{1,0:T(8,128)(2,1)S(1)}, bf16[256,2304]{1,0:T(8,128)(2,1)}, u32[]{:S(2)}) copy-start(bf16[256,2304]{1,0:T(8,128)(2,1)} %param.16) | copy-start | bytes 3538948
  (22 other events, 63.2 us)
Sparse Core Ops, SparseCore 0:
  105.2 55.0 all-gather.7

commit v2 on v1

--- a/solution.py
+++ b/solution.py
@@ -1,15 +1,93 @@
 import jax
 import jax.numpy as jnp
 from jax import lax
+from jax.experimental import pallas as pl
+from jax.experimental.pallas import tpu as pltpu
 from jax.sharding import PartitionSpec as P
 
 HD = 64
 CAP = 80
 CHUNKS = 4
+GROUP = 384
+PAIR = 2 * HD
 
 NEG_FILL = -1e30
 SCORE_SCALE = 0.125
 EPSILON = 1e-05
+
+
+def attend_kernel(valid_ref, causal_ref, query_ref, cache_ref, new_ref, numer_ref, stats_ref):
+    slots, page = cache_ref.shape[1], cache_ref.shape[3]
+    heads = GROUP // HD
+    rows = query_ref.shape[1]
+    valid = valid_ref[0] > 0
+    causal = causal_ref[...] > 0
+    lower = lax.broadcasted_iota(jnp.int32, (rows, PAIR), 1) < HD
+    nt = (((1,), (1,)), ((), ()))
+    for pair in range(GROUP // PAIR):
+        cols = slice(pair * PAIR, (pair + 1) * PAIR)
+        query = query_ref[0, :, cols]
+        keys = cache_ref[0, :, 0, :, cols].reshape(slots * page, PAIR)
+        vals = cache_ref[0, :, 1, :, cols].reshape(slots * page, PAIR)
+        new_keys = new_ref[0, 0, :, cols]
+        new_vals = new_ref[0, 1, :, cols]
+        sums = []
+        for side in range(2):
+            own = jnp.where(lower if side == 0 else ~lower, query, jnp.zeros_like(query))
+            far = lax.dot_general(own, keys, nt, preferred_element_type=jnp.float32)
+            near = lax.dot_general(own, new_keys, nt, preferred_element_type=jnp.float32)
+            far = jnp.where(valid, far * SCORE_SCALE, NEG_FILL)
+            near = jnp.where(causal, near * SCORE_SCALE, NEG_FILL)
+            top = jnp.maximum(
+                jnp.max(far, axis=1, keepdims=True), jnp.max(near, axis=1, keepdims=True)
+            )
+            far = jnp.where(valid, jnp.exp(far - top), 0.0)
+            near = jnp.where(causal, jnp.exp(near - top), 0.0)
+            total = jnp.sum(far, axis=1, keepdims=True) + jnp.sum(near, axis=1, keepdims=True)
+            sums.append(
+                jnp.dot(far.astype(jnp.bfloat16), vals, preferred_element_type=jnp.float32)
+                + jnp.dot(near.astype(jnp.bfloat16), new_vals, preferred_element_type=jnp.float32)
+            )
+            head = 2 * pair + side
+            stats_ref[0, 0, :, head : head + 1] = top
+            stats_ref[0, 0, :, heads + head : heads + head + 1] = total
+        numer_ref[0, :, cols] = jnp.where(lower, sums[0], sums[1]).astype(jnp.bfloat16)
+
+
+def attend(queries, new_kv, cache_pool, cache_valid, new_valid):
+    reqs, rows, width = queries.shape
+    slots, page = cache_pool.shape[1], cache_pool.shape[3]
+    new_rows = new_kv.shape[2]
+    groups = width // GROUP
+    heads = GROUP // HD
+    numer, stats = pl.pallas_call(
+        attend_kernel,
+        grid=(reqs, groups),
+        in_specs=[
+            pl.BlockSpec((1, 1, slots * page), lambda r, g: (r, 0, 0)),
+            pl.BlockSpec((rows, new_rows), lambda r, g: (0, 0)),
+            pl.BlockSpec((1, rows, GROUP), lambda r, g: (r, 0, g)),
+            pl.BlockSpec((1, slots, 2, page, GROUP), lambda r, g: (r, 0, 0, 0, g)),
+            pl.BlockSpec((1, 2, new_rows, GROUP), lambda r, g: (r, 0, 0, g)),
+        ],
+        out_specs=[
+            pl.BlockSpec((1, rows, GROUP), lambda r, g: (r, 0, g)),
+            pl.BlockSpec((1, 1, rows, 2 * heads), lambda r, g: (r, g, 0, 0)),
+        ],
+        out_shape=[
+            jax.ShapeDtypeStruct((reqs, rows, width), jnp.bfloat16),
+            jax.ShapeDtypeStruct((reqs, groups, rows, 2 * heads), jnp.float32),
+        ],
+        compiler_params=pltpu.CompilerParams(vmem_limit_bytes=32 * 2**20),
+    )(
+        cache_valid.astype(jnp.float32)[:, None, :],
+        new_valid.astype(jnp.float32),
+        queries,
+        cache_pool,
+        new_kv,
+    )
+    stats = stats.reshape(reqs, groups, rows, 2, heads).transpose(3, 0, 1, 4, 2)
+    return numer, stats.reshape(2, reqs, groups * heads, rows)
 
 
 def local(
@@ -34,11 +112,6 @@
     page_len = cache_pool.shape[3]
     local_new = new_kv.shape[2]
     table_len = page_table.shape[1]
-    query_heads = queries.reshape(req_here, new_len, head_count, HD)
-    cache_keys = cache_pool[:, :, 0].reshape(req_here, slot_count * page_len, head_count, HD)
-    cache_vals = cache_pool[:, :, 1].reshape(req_here, slot_count * page_len, head_count, HD)
-    new_keys = new_kv[:, 0].reshape(req_here, local_new, head_count, HD)
-    new_vals = new_kv[:, 1].reshape(req_here, local_new, head_count, HD)
     own_slots = narrow_pos * slot_count + jnp.arange(slot_count, dtype=jnp.int32)
     matches = page_table[:, None, :] == own_slots[None, :, None]
     logical = jnp.sum(
@@ -48,36 +121,13 @@
     cache_valid = key_pos.reshape(req_here, slot_count * page_len) < cached_len[:, None]
     new_pos = narrow_pos * local_new + jnp.arange(local_new, dtype=jnp.int32)
     new_valid = new_pos[None, :] <= jnp.arange(new_len, dtype=jnp.int32)[:, None]
-    cache_scores = (
-        jnp.einsum("rqhd,rkhd->rhqk", query_heads, cache_keys, preferred_element_type=jnp.float32)
-        * SCORE_SCALE
-    )
-    new_scores = (
-        jnp.einsum("rqhd,rkhd->rhqk", query_heads, new_keys, preferred_element_type=jnp.float32)
-        * SCORE_SCALE
-    )
-    cache_scores = jnp.where(cache_valid[:, None, None, :], cache_scores, NEG_FILL)
-    new_scores = jnp.where(new_valid[None, None], new_scores, NEG_FILL)
-    own_top = jnp.maximum(jnp.max(cache_scores, axis=3), jnp.max(new_scores, axis=3))
-    cache_weights = jnp.where(
-        cache_valid[:, None, None, :], jnp.exp(cache_scores - own_top[..., None]), 0.0
-    )
-    new_weights = jnp.where(new_valid[None, None], jnp.exp(new_scores - own_top[..., None]), 0.0)
-    denominator = jnp.sum(cache_weights, axis=3) + jnp.sum(new_weights, axis=3)
-    numerator = jnp.einsum(
-        "rhqk,rkhd->rqhd",
-        cache_weights.astype(jnp.bfloat16),
-        cache_vals,
-        preferred_element_type=jnp.float32,
-    )
-    numerator = numerator + jnp.einsum(
-        "rhqk,rkhd->rqhd",
-        new_weights.astype(jnp.bfloat16),
-        new_vals,
-        preferred_element_type=jnp.float32,
-    )
-    numerator = numerator.reshape(req_here * new_len, model_width).astype(jnp.bfloat16)
-    stats = jnp.stack([own_top, denominator])
+    numerator, stats = attend(
+        queries,
+        new_kv,
+        cache_pool,
+        cache_valid.reshape(req_here, slot_count * page_len),
+        new_valid,
+    )
     stats = lax.all_gather(stats, "narrow", axis=0)
     feature_count = model_width // narrow_count
     token_rows = req_here * new_len
@@ -102,8 +152,12 @@
     scale = lax.rsqrt(squares / model_width + EPSILON)
     normed = (all_rows.astype(jnp.float32) * scale[:, :, None]).astype(jnp.bfloat16)
 
-    all_ids = lax.all_gather(expert_ids, "wide", axis=0)
-    all_route = lax.all_gather(route_weight, "wide", axis=0)
+    routing = jnp.concatenate(
+        [expert_ids.astype(jnp.float32).reshape(-1), route_weight.reshape(-1)]
+    )
+    routing = lax.all_gather(routing, "wide", axis=0).reshape(wide_count, 2, token_rows, 2)
+    all_ids = routing[:, 0].astype(jnp.int32)
+    all_route = routing[:, 1]
     chips = narrow_count // 2
     chip, core = narrow_pos // 2, narrow_pos % 2
     block = wide_count // narrow_count
@@ -148,17 +202,24 @@
     rows_half = wide_count * CAP // 2
     rows_own = rows_half // chips
     out_chunks = []
+    sents, owns = [], []
     for chunk in range(CHUNKS):
         picked = slice(chunk * per_chunk, (chunk + 1) * per_chunk)
+        rows_in = placed[picked]
+        if chunk >= 2:
+            rows_in, sents[chunk - 2] = lax.optimization_barrier((rows_in, sents[chunk - 2]))
         partial = jnp.einsum(
-            "erd,gedf->gerf", placed[picked], table[:, picked], preferred_element_type=jnp.float32
+            "erd,gedf->gerf", rows_in, table[:, picked], preferred_element_type=jnp.float32
         ).astype(jnp.bfloat16)
         near = lax.ppermute(partial[:, :, rows_half:], "narrow", core_pairs)
         both = (
             partial[:, :, :rows_half].astype(jnp.float32) + near.astype(jnp.float32)
         )
-        own = both[:, :, :rows_own]
-        sent = both[:, :, rows_own:].astype(jnp.bfloat16)
+        owns.append(both[:, :, :rows_own])
+        sents.append(both[:, :, rows_own:].astype(jnp.bfloat16))
+    for chunk in range(CHUNKS):
+        picked = slice(chunk * per_chunk, (chunk + 1) * per_chunk)
+        own, sent = owns[chunk], sents[chunk]
         for step in range(1, chips):
             arrived = lax.ppermute(
                 sent[:, :, (step - 1) * rows_own : step * rows_own], "narrow", chip_pairs(step)
@@ -170,6 +231,8 @@
         ]
         mine = jnp.concatenate(mine, axis=1)
         other = lax.ppermute(mine, "narrow", core_pairs)
+        if out_chunks:
+            other, out_chunks[-1] = lax.optimization_barrier((other, out_chunks[-1]))
         whole = jnp.concatenate([mine, other], axis=1)
         out_chunks.append(
             jnp.einsum(

time: 524 us -> 455 us (0.87)
  local copies, waits for them, and re-layouts: 116 us -> 83 us
  Pallas kernels: 0 us -> 25.4 us
  waiting for transfers between devices: 104 us -> 81.1 us
  matrix products: 64.2 us -> 42.4 us
  blocking collectives: 157 us -> 148 us
    pallas_call x0 -> x1, Pallas kernels: none -> 25.4 us  [attend(): pl.pallas_call(attend_kernel, grid=(reqs, groups), in_specs=[pl.BlockSpec...]
    dot_general x8 -> x4, matrix products: 36 us -> 13.9 us  [local(): jnp.einsum('erd,gedf->gerf', rows_in, table[:, picked], preferred_element...]
    slice x14 -> x9, local copies, waits for them, and re-layouts: 27.9 us -> 5.9 us  [the longest x4 4.62 us: local(): sents.append(both[:, :, rows_own:].astype(jnp.bfloat16))]
    all_gather x2 -> x1, blocking collectives: 53.4 us -> 31.8 us  [local(): lax.all_gather(routing, 'wide', axis=0)]
    another operation x4 -> x0, local copies, waits for them, and re-layouts: 18.8 us -> none  [the longest x1 8.14 us: local(): cache_pool[:, :, 0].reshape(req_here, slot_count * page_len, head_count, HD)]
    ppermute x4, waiting for transfers between devices: 28.7 us -> 12.6 us  [local(): lax.ppermute(active, 'narrow', chip_pairs(chips - step))]
    all_gather x1, blocking collectives: 7.4 us -> 18 us  [local(): stats = lax.all_gather(stats, 'narrow', axis=0)]
    reduce_sum x2 -> x1, other arithmetic: 10.3 us -> 0.13 us  [local(): factor = factor / jnp.sum(factor * dens, axis=0, keepdims=True)]
  transfers between devices with their start and end apart: 18 -> 18, of which waited for: 7 -> 8; matrix products, arithmetic and copies ran while one was open for 19% -> 22% of each run, Pallas kernels for 0% -> 0%
where the time goes in v2:
time: 455 us; the launch traced here: 448 us
  blocking collectives  148 us (33%)
  local copies, waits for them, and re-layouts  83 us (18%)
  waiting for transfers between devices  81.1 us (18%)
  other arithmetic  43.8 us (10%)
  matrix products  42.4 us (9%)
  Pallas kernels  25.4 us (6%)
  between operations  14.5 us (3%)
  starting transfers between devices  10.3 us (2%)
    ppermute x4, waiting for transfers between devices, local(): lax.ppermute(sent[:, :, (step - 1) * rows_own:step * rows_own], 'narrow',...  67.9 us
    all_to_all x1, blocking collectives, local(): mixed = lax.all_to_all(mixed[back], 'wide', 0, 0)  57.3 us
    all_gather x1, blocking collectives, local(): lax.all_gather(jnp.sum(hidden * hidden, axis=1), ('wide', 'narrow'), axis=0)  40.8 us
    all_gather x1, blocking collectives, local(): lax.all_gather(routing, 'wide', axis=0)  31.8 us
    unnamed x66, local copies, waits for them, and re-layouts  26.5 us
    pallas_call x1, Pallas kernels, attend(): pl.pallas_call(attend_kernel, grid=(reqs, groups), in_specs=[pl.BlockSpec...  25.4 us
    all_gather x1, blocking collectives, local(): stats = lax.all_gather(stats, 'narrow', axis=0)  18 us
    dot_general x4, matrix products, local(): jnp.einsum('erf,efd->erd', whole, w_down[picked], preferred_element_type=...  16.1 us
  transfers between devices with their start and end apart: 18, of which 8 were waited for; matrix products, arithmetic and copies ran while one was open for 22% of the time, Pallas kernels for 0%

profile of v2, /device:TPU:0, one launch (start us, length us, event | category | flops | bytes accessed | tf_op | source)
XLA Modules:
  0.0 448.4 jit_solution(3736103061927741567)
XLA Ops:
  8.3 3.7 copy-done.2
  14.4 25.4 %shard_map.109 = (bf16[2,128,2304]{2,1,0:T(8,128)(2,1)S(1)}, f32[2,6,128,12]{3,2,1,0:T(8,128)S(1)}) custom-call(f32[2,1,512]{2,1,0:T(1,128)S(1)} %compare_convert_fusion.valid_ref, f32[128,32]{1,0:T(8,128)S(1)} %fusion.92.causal_ref, bf16[2,128,2304]{2,1,0:T(8,128)(2,1)S(1)} %copy-done.3, bf16[2,4,2,128,2304]{4,3,2,1,0:T(8,128)(2,1)S(1)} %copy-done.2, ...), custom_call_target="tpu_custom_call" | custom-call | tf_op jit(solution)/shard_map/pallas_call | solution.py:63
  39.8 2.4 reshape.292
  42.2 3.4 copy.309
  45.7 4.2 all-to-all-start
  50.1 18.0 %all_gather.21 = f32[4,2,2,36,128]{4,2,3,1,0:T(2,128)S(1)} all-gather(f32[1,2,2,36,128]{4,2,3,1,0:T(2,128)S(1)} %bitcast.150), channel_id=1, replica_groups=mesh['wide'=8,'narrow'=4] {'narrow'}, dimensions={0}, use_global_device_ids=true | all-gather | bytes 368640 | tf_op jit(solution)/shard_map/all_gather | solution.py:131
  72.6 31.8 %all-gather = f32[8192]{0:T(1024)S(1)} all-gather(f32[1024]{0:T(1024)S(1)} %pad_maximum_fusion.5), channel_id=2, replica_groups=mesh['wide'=8,'narrow'=4] {'wide'}, dimensions={0}, use_global_device_ids=true | all-gather | bytes 36864 | tf_op jit(solution)/shard_map/all_gather | solution.py:158
  111.3 8.8 %copy.346 = bf16[8,576,2,720]{3,1,2,0:T(8,128)(2,1)S(1)} copy(bf16[8,576,2,720]{3,2,1,0:T(2,128)(2,1)} %param.20) | data formatting | bytes 26542080 | tf_op args[9]
  120.1 7.1 %fusion = pred[8,640,256]{2,1,0:T(8,128)(4,1)} fusion(s32[8,256,2]{1,2,0:T(2,128)S(1)} %copy.265), kind=kLoop, calls=%fused_computation.7 | loop fusion | flops 3932160 | bytes 1327104 | tf_op jit(solution)/shard_map/reduce_or | solution.py:184
  127.2 5.2 %fusion.110 = (bf16[2,2,576,720]{3,2,0,1:T(8,128)(2,1)}, bf16[2,2,576,720]{3,2,0,1:T(8,128)(2,1)}, bf16[2,2,576,720]{3,2,0,1:T(8,128)(2,1)}, bf16[2,2,576,720]{3,2,0,1:T(8,128)(2,1)}) fusion(bf16[2,8,576,720]{3,2,0,1:T(8,128)(2,1)S(1)} %bitcast.138), kind=kLoop, calls=%fused_computation.169 | loop fusion | bytes 26542080 | tf_op jit(solution)/shard_map/slice | solution.py:212
  132.4 40.8 %all-gather.3 = f32[32,1,256]{2,1,0:T(1,128)S(1)} all-gather(f32[1,1,256]{2,1,0:T(1,128)S(1)} %bitcast.152), channel_id=4, replica_groups=mesh['wide'=8,'narrow'=4] {'wide','narrow'}, dimensions={0}, use_global_device_ids=true | all-gather | bytes 33792 | tf_op jit(solution)/shard_map/all_gather | solution.py:149
  177.4 2.4 gather_fusion.2
  179.8 3.5 convert_bitcast_fusion
  185.3 3.4 convert_bitcast_fusion.4
  190.7 3.4 convert_bitcast_fusion.3
  201.7 3.5 convert_bitcast_fusion.2
  209.3 3.6 convert_bitcast_fusion.1
  216.4 10.1 %collective-permute-done.1 = bf16[2,2,160,720]{3,2,1,0:T(8,128)(2,1)S(1)} collective-permute-done((bf16[2,2,160,720]{3,2,1,0:T(8,128)(2,1)}, bf16[2,2,160,720]{3,2,1,0:T(8,128)(2,1)S(1)}, u32[]{:S(2)}, u32[]{:S(2)}) %collective-permute-start.1) | collective-permute-done | bytes 921632 | tf_op jit(solution)/shard_map/ppermute | solution.py:224
  228.8 18.9 %collective-permute-done.5 = bf16[2,2,160,720]{3,2,1,0:T(8,128)(2,1)} collective-permute-done((bf16[2,2,160,720]{3,2,1,0:T(8,128)(2,1)}, bf16[2,2,160,720]{3,2,1,0:T(8,128)(2,1)}, u32[]{:S(2)}, u32[]{:S(2)}) %collective-permute-start.5) | collective-permute-done | bytes 921632 | tf_op jit(solution)/shard_map/ppermute | solution.py:224
  260.8 3.3 select_reduce_fusion
  269.7 20.0 %collective-permute-done.9 = bf16[2,2,160,720]{3,2,1,0:T(8,128)(2,1)S(1)} collective-permute-done((bf16[2,2,160,720]{3,2,1,0:T(8,128)(2,1)}, bf16[2,2,160,720]{3,2,1,0:T(8,128)(2,1)S(1)}, u32[]{:S(2)}, u32[]{:S(2)}) %collective-permute-start.9) | collective-permute-done | bytes 921632 | tf_op jit(solution)/shard_map/ppermute | solution.py:224
  292.0 18.9 %collective-permute-done.13 = bf16[2,2,160,720]{3,2,1,0:T(8,128)(2,1)} collective-permute-done((bf16[2,2,160,720]{3,2,1,0:T(8,128)(2,1)}, bf16[2,2,160,720]{3,2,1,0:T(8,128)(2,1)}, u32[]{:S(2)}, u32[]{:S(2)}) %collective-permute-start.13) | collective-permute-done | bytes 921632 | tf_op jit(solution)/shard_map/ppermute | solution.py:224
  319.0 2.4 collective-permute-done.10
  323.5 7.9 %collective-permute-done.14 = bf16[2,160,720]{2,1,0:T(8,128)(2,1)} collective-permute-done((bf16[2,160,720]{2,1,0:T(8,128)(2,1)S(1)}, bf16[2,160,720]{2,1,0:T(8,128)(2,1)}, u32[]{:S(2)}, u32[]{:S(2)}) %collective-permute-start.14) | collective-permute-done | bytes 460832 | tf_op jit(solution)/shard_map/ppermute | solution.py:230
  333.4 4.3 fusion.66
  339.6 4.7 %fusion.61 = bf16[2,640,576]{1,2,0:T(8,128)(2,1)} fusion(bf16[2,320,720]{1,2,0:T(8,128)(2,1)S(1)} %copy.284, bf16[2,160,720]{1,2,0:T(8,128)(2,1)} %copy.283, bf16[2,160,720]{1,2,0:T(8,128)(2,1)} %copy.282, bf16[8,720,576]{1,2,0:T(8,128)(2,1)} %param.21), kind=kOutput, calls=%fused_computation.72 | convolution fusion | flops 1067950080 | bytes 5640192 | tf_op jit(solution)/shard_map/erf,efd->erd/dot_general | solution.py:238
  351.6 3.6 fusion.56
  356.9 3.5 fusion.51
  360.4 3.2 pad_maximum_fusion
  363.6 8.6 %copy.293 = bf16[8,640,576]{2,1,0:T(8,128)(2,1)} copy(bf16[8,640,576]{1,2,0:T(8,128)(2,1)} %pad_maximum_fusion) | data formatting | bytes 11796480 | tf_op jit(solution)/shard_map/concatenate | solution.py:242
  372.2 7.4 %bitcast_convert_fusion = bf16[8,256,576]{1,2,0:T(8,128)(2,1)} fusion(bf16[8,8,80,256]{3,2,1,0:T(8,128)(2,1)} %bitcast.142, bf16[8,8,80,576]{3,2,1,0:T(8,128)(2,1)} %bitcast.140), kind=kOutput, calls=%fused_computation.14 | convolution fusion | flops 1511129088 | bytes 10878976 | tf_op jit(solution)/shard_map/wect,ewcd->wtd/dot_general | solution.py:245
  382.0 57.3 %all_to_all.10 = bf16[8,256,576]{1,2,0:T(8,128)(2,1)S(1)} all-to-all(bf16[8,256,576]{1,2,0:T(8,128)(2,1)S(1)} %gather_fusion.3), channel_id=1, replica_groups=mesh['wide'=8,'narrow'=4] {'wide'}, dimensions={0} | all-to-all | bytes 4718592 | tf_op jit(solution)/shard_map/all_to_all | solution.py:249
  (191 shorter events, 89.2 us)
Async XLA Ops:
  6.5 62.1 %copy-start = (bf16[256,2304]{1,0:T(8,128)(2,1)S(1)}, bf16[256,2304]{1,0:T(8,128)(2,1)}, u32[]{:S(2)}) copy-start(bf16[256,2304]{1,0:T(8,128)(2,1)} %param.16) | copy-start | bytes 3538948
  8.3 3.7 copy-start.2
  45.7 24.2 %all-to-all-start = ((bf16[4,256,576]{1,2,0:T(8,128)(2,1)}), bf16[4,256,576]{1,2,0:T(8,128)(2,1)S(1)}, u32[]{:S(2)}, u32[]{:S(2)}) async-start(bf16[4,256,576]{1,2,0:T(8,128)(2,1)} %bitcast.2), calls=%async_computation | async-start | bytes 2359296 | tf_op jit(solution)/shard_map/all_to_all | solution.py:135
  49.9 123.4 %all-gather.6.cloned.1.call-start = ((), (), s32[]{:S(2)}) async-start(), calls=%async_computation.2 | async-start | bytes 2654208 | tf_op jit(solution)/shard_map/all_gather | solution.py:150
  69.0 37.6 %copy-start.22 = (bf16[256,576]{0,1:T(8,128)(2,1)}, bf16[256,576]{0,1:T(8,128)(2,1)S(1)}, u32[]{:S(2)}) copy-start(bf16[256,576]{0,1:T(8,128)(2,1)S(1)} %copy.316) | copy-start | bytes 884740
  71.0 37.2 %copy-start.11 = (f32[256,576]{0,1:T(8,128)}, f32[256,576]{0,1:T(8,128)S(1)}, u32[]{:S(2)}) copy-start(f32[256,576]{0,1:T(8,128)S(1)} %multiply_reduce_fusion) | copy-start | bytes 1769476
  188.9 6.1 %collective-permute-start = (bf16[2,2,320,720]{3,2,1,0:T(8,128)(2,1)S(1)}, bf16[2,2,320,720]{3,2,1,0:T(8,128)(2,1)S(1)}, u32[]{:S(2)}, u32[]{:S(2)}) collective-permute-start(bf16[2,2,320,720]{3,2,1,0:T(8,128)(2,1)S(1)} %slice.195), channel_id=1, source_target_pairs={{0,1},{1,0},{2,3},{3,2},{4,5},{5,4},{6,7},{7,6},{8,9},{9,8},{10,11... | collective-permute-start | bytes 5529608 | tf_op jit(solution)/shard_map/ppermute | solution.py:214
  194.3 4.0 collective-permute-start.4
  197.7 4.0 copy-start.19
  201.7 24.8 %collective-permute-start.1 = (bf16[2,2,160,720]{3,2,1,0:T(8,128)(2,1)}, bf16[2,2,160,720]{3,2,1,0:T(8,128)(2,1)S(1)}, u32[]{:S(2)}, u32[]{:S(2)}) collective-permute-start(bf16[2,2,160,720]{3,2,1,0:T(8,128)(2,1)} %slice.300), channel_id=1, source_target_pairs={{0,2},{1,3},{2,0},{3,1},{4,6},{5,7},{6,4},{7,5},{8,10},{9,11},{10,... | collective-permute-start | bytes 2764808 | tf_op jit(solution)/shard_map/ppermute | solution.py:224
  205.2 7.8 %copy-start.14 = (bf16[2,2,640,720]{3,2,1,0:T(8,128)(2,1)}, bf16[2,2,640,720]{3,2,1,0:T(8,128)(2,1)S(1)}, u32[]{:S(2)}) copy-start(bf16[2,2,640,720]{3,2,1,0:T(8,128)(2,1)S(1)} %convert_bitcast_fusion.2) | copy-start | bytes 11059204
  205.2 4.1 copy-start.18
  206.6 43.0 %collective-permute-start.8 = (bf16[2,2,320,720]{3,2,1,0:T(8,128)(2,1)}, bf16[2,2,320,720]{3,2,1,0:T(8,128)(2,1)}, u32[]{:S(2)}, u32[]{:S(2)}) collective-permute-start(bf16[2,2,320,720]{3,2,1,0:T(8,128)(2,1)} %slice.212), channel_id=1, source_target_pairs={{0,1},{1,0},{2,3},{3,2},{4,5},{5,4},{6,7},{7,6},{8,9},{9,8},{10,11... | collective-permute-start | bytes 5529608 | tf_op jit(solution)/shard_map/ppermute | solution.py:214
  207.0 40.7 %collective-permute-start.5 = (bf16[2,2,160,720]{3,2,1,0:T(8,128)(2,1)}, bf16[2,2,160,720]{3,2,1,0:T(8,128)(2,1)}, u32[]{:S(2)}, u32[]{:S(2)}) collective-permute-start(bf16[2,2,160,720]{3,2,1,0:T(8,128)(2,1)} %slice.299), channel_id=1, source_target_pairs={{0,2},{1,3},{2,0},{3,1},{4,6},{5,7},{6,4},{7,5},{8,10},{9,11},{10,... | collective-permute-start | bytes 2764808 | tf_op jit(solution)/shard_map/ppermute | solution.py:224
  214.4 40.6 %collective-permute-start.12 = (bf16[2,2,320,720]{3,2,1,0:T(8,128)(2,1)}, bf16[2,2,320,720]{3,2,1,0:T(8,128)(2,1)}, u32[]{:S(2)}, u32[]{:S(2)}) collective-permute-start(bf16[2,2,320,720]{3,2,1,0:T(8,128)(2,1)} %slice.219), channel_id=1, source_target_pairs={{0,1},{1,0},{2,3},{3,2},{4,5},{5,4},{6,7},{7,6},{8,9},{9,8},{10,11... | collective-permute-start | bytes 5529608 | tf_op jit(solution)/shard_map/ppermute | solution.py:214
  226.5 21.2 %copy-start.8 = (f32[2,2,320,720]{3,2,1,0:T(8,128)S(1)}, f32[2,2,320,720]{3,2,1,0:T(8,128)}, u32[]{:S(2)}) copy-start(f32[2,2,320,720]{3,2,1,0:T(8,128)} %copy-done.7) | copy-start | bytes 11059204
  228.7 36.5 %collective-permute-start.2 = (bf16[2,160,720]{2,1,0:T(8,128)(2,1)S(1)}, bf16[2,160,720]{2,1,0:T(8,128)(2,1)S(1)}, u32[]{:S(2)}, u32[]{:S(2)}) collective-permute-start(bf16[2,160,720]{2,1,0:T(8,128)(2,1)S(1)} %fusion.84), channel_id=1, source_target_pairs={{0,2},{1,3},{2,0},{3,1},{4,6},{5,7},{6,4},{7,5},{8,10},{9,11},{10,... | collective-permute-start | bytes 1382408 | tf_op jit(solution)/shard_map/ppermute | solution.py:230
  249.6 19.0 %collective-permute-start.6 = (bf16[2,160,720]{2,1,0:T(8,128)(2,1)S(1)}, bf16[2,160,720]{2,1,0:T(8,128)(2,1)S(1)}, u32[]{:S(2)}, u32[]{:S(2)}) collective-permute-start(bf16[2,160,720]{2,1,0:T(8,128)(2,1)S(1)} %fusion.82), channel_id=1, source_target_pairs={{0,2},{1,3},{2,0},{3,1},{4,6},{5,7},{6,4},{7,5},{8,10},{9,11},{10,... | collective-permute-start | bytes 1382408 | tf_op jit(solution)/shard_map/ppermute | solution.py:230
  250.1 4.9 %copy-start.17 = (bf16[2,2,640,720]{3,2,1,0:T(8,128)(2,1)S(1)}, bf16[2,2,640,720]{3,2,1,0:T(8,128)(2,1)}, u32[]{:S(2)}) copy-start(bf16[2,2,640,720]{3,2,1,0:T(8,128)(2,1)} %copy-done.16) | copy-start | bytes 11059204
  253.4 36.3 %collective-permute-start.9 = (bf16[2,2,160,720]{3,2,1,0:T(8,128)(2,1)}, bf16[2,2,160,720]{3,2,1,0:T(8,128)(2,1)S(1)}, u32[]{:S(2)}, u32[]{:S(2)}) collective-permute-start(bf16[2,2,160,720]{3,2,1,0:T(8,128)(2,1)} %slice.298), channel_id=1, source_target_pairs={{0,2},{1,3},{2,0},{3,1},{4,6},{5,7},{6,4},{7,5},{8,10},{9,11},{10,... | collective-permute-start | bytes 2764808 | tf_op jit(solution)/shard_map/ppermute | solution.py:224
  259.9 51.0 %collective-permute-start.13 = (bf16[2,2,160,720]{3,2,1,0:T(8,128)(2,1)}, bf16[2,2,160,720]{3,2,1,0:T(8,128)(2,1)}, u32[]{:S(2)}, u32[]{:S(2)}) collective-permute-start(bf16[2,2,160,720]{3,2,1,0:T(8,128)(2,1)} %slice.297), channel_id=1, source_target_pairs={{0,2},{1,3},{2,0},{3,1},{4,6},{5,7},{6,4},{7,5},{8,10},{9,11},{10,... | collective-permute-start | bytes 2764808 | tf_op jit(solution)/shard_map/ppermute | solution.py:224
  266.3 71.4 %collective-permute-start.3 = (bf16[2,320,720]{2,1,0:T(8,128)(2,1)}, bf16[2,320,720]{2,1,0:T(8,128)(2,1)}, u32[]{:S(2)}, u32[]{:S(2)}) collective-permute-start(bf16[2,320,720]{2,1,0:T(8,128)(2,1)} %pad_maximum_fusion.1), channel_id=1, source_target_pairs={{0,1},{1,0},{2,3},{3,2},{4,5},{5,4},{6,7},{7,6},{8,9},{9,8},{10,11... | collective-permute-start | bytes 2764808 | tf_op jit(solution)/shard_map/ppermute | solution.py:233
  269.7 47.7 %collective-permute-start.7 = (bf16[2,320,720]{2,1,0:T(8,128)(2,1)}, bf16[2,320,720]{2,1,0:T(8,128)(2,1)}, u32[]{:S(2)}, u32[]{:S(2)}) collective-permute-start(bf16[2,320,720]{2,1,0:T(8,128)(2,1)} %pad_maximum_fusion.2), channel_id=1, source_target_pairs={{0,1},{1,0},{2,3},{3,2},{4,5},{5,4},{6,7},{7,6},{8,9},{9,8},{10,11... | collective-permute-start | bytes 2764808 | tf_op jit(solution)/shard_map/ppermute | solution.py:233
  289.7 21.2 %copy-start.6 = (f32[2,2,320,720]{3,2,1,0:T(8,128)S(1)}, f32[2,2,320,720]{3,2,1,0:T(8,128)}, u32[]{:S(2)}) copy-start(f32[2,2,320,720]{3,2,1,0:T(8,128)} %copy-done.5) | copy-start | bytes 11059204
  291.9 29.5 %collective-permute-start.10 = (bf16[2,160,720]{2,1,0:T(8,128)(2,1)S(1)}, bf16[2,160,720]{2,1,0:T(8,128)(2,1)}, u32[]{:S(2)}, u32[]{:S(2)}) collective-permute-start(bf16[2,160,720]{2,1,0:T(8,128)(2,1)S(1)} %fusion.80), channel_id=1, source_target_pairs={{0,2},{1,3},{2,0},{3,1},{4,6},{5,7},{6,4},{7,5},{8,10},{9,11},{10,... | collective-permute-start | bytes 1382408 | tf_op jit(solution)/shard_map/ppermute | solution.py:230
  312.7 18.7 %collective-permute-start.14 = (bf16[2,160,720]{2,1,0:T(8,128)(2,1)S(1)}, bf16[2,160,720]{2,1,0:T(8,128)(2,1)}, u32[]{:S(2)}, u32[]{:S(2)}) collective-permute-start(bf16[2,160,720]{2,1,0:T(8,128)(2,1)S(1)} %fusion.78), channel_id=1, source_target_pairs={{0,2},{1,3},{2,0},{3,1},{4,6},{5,7},{6,4},{7,5},{8,10},{9,11},{10,... | collective-permute-start | bytes 1382408 | tf_op jit(solution)/shard_map/ppermute | solution.py:230
  319.0 14.4 %copy-start.26 = (bf16[2,160,720]{1,2,0:T(8,128)(2,1)S(1)}, bf16[2,160,720]{1,2,0:T(8,128)(2,1)}, u32[]{:S(2)}) copy-start(bf16[2,160,720]{1,2,0:T(8,128)(2,1)} %copy.277) | copy-start | bytes 1382404
  319.0 14.4 %copy-start.27 = (bf16[2,160,720]{1,2,0:T(8,128)(2,1)S(1)}, bf16[2,160,720]{1,2,0:T(8,128)(2,1)}, u32[]{:S(2)}) copy-start(bf16[2,160,720]{1,2,0:T(8,128)(2,1)} %copy.278) | copy-start | bytes 1382404
  323.5 27.4 %collective-permute-start.11 = (bf16[2,320,720]{2,1,0:T(8,128)(2,1)}, bf16[2,320,720]{2,1,0:T(8,128)(2,1)S(1)}, u32[]{:S(2)}, u32[]{:S(2)}) collective-permute-start(bf16[2,320,720]{2,1,0:T(8,128)(2,1)} %pad_maximum_fusion.3), channel_id=1, source_target_pairs={{0,1},{1,0},{2,3},{3,2},{4,5},{5,4},{6,7},{7,6},{8,9},{9,8},{10,11... | collective-permute-start | bytes 2764808 | tf_op jit(solution)/shard_map/ppermute | solution.py:233
  333.4 21.8 %collective-permute-start.15 = (bf16[2,320,720]{2,1,0:T(8,128)(2,1)}, bf16[2,320,720]{2,1,0:T(8,128)(2,1)}, u32[]{:S(2)}, u32[]{:S(2)}) collective-permute-start(bf16[2,320,720]{2,1,0:T(8,128)(2,1)} %pad_maximum_fusion.4), channel_id=1, source_target_pairs={{0,1},{1,0},{2,3},{3,2},{4,5},{5,4},{6,7},{7,6},{8,9},{9,8},{10,11... | collective-permute-start | bytes 2764808 | tf_op jit(solution)/shard_map/ppermute | solution.py:233
  351.6 5.3 %copy-start.28 = (bf16[2,160,720]{1,2,0:T(8,128)(2,1)S(1)}, bf16[2,160,720]{1,2,0:T(8,128)(2,1)}, u32[]{:S(2)}) copy-start(bf16[2,160,720]{1,2,0:T(8,128)(2,1)} %copy.290) | copy-start | bytes 1382404
  382.0 59.3 %copy-start.1 = (bf16[256,2304]{1,0:T(8,128)(2,1)S(1)}, bf16[256,2304]{1,0:T(8,128)(2,1)}, u32[]{:S(2)}) copy-start(bf16[256,2304]{1,0:T(8,128)(2,1)} %param.16) | copy-start | bytes 3538948
  (17 other events, 39.0 us)
Sparse Core Ops, SparseCore 0:
  72.1 55.7 all-gather.5

commit v3 on v2

--- a/solution.py
+++ b/solution.py
@@ -201,7 +201,7 @@
     per_chunk = expert_count // CHUNKS
     rows_half = wide_count * CAP // 2
     rows_own = rows_half // chips
-    out_chunks = []
+    total = None
     sents, owns = [], []
     for chunk in range(CHUNKS):
         picked = slice(chunk * per_chunk, (chunk + 1) * per_chunk)
@@ -231,20 +231,20 @@
         ]
         mine = jnp.concatenate(mine, axis=1)
         other = lax.ppermute(mine, "narrow", core_pairs)
-        if out_chunks:
-            other, out_chunks[-1] = lax.optimization_barrier((other, out_chunks[-1]))
+        if total is not None:
+            other, total = lax.optimization_barrier((other, total))
         whole = jnp.concatenate([mine, other], axis=1)
-        out_chunks.append(
-            jnp.einsum(
-                "erf,efd->erd", whole, w_down[picked], preferred_element_type=jnp.float32
-            ).astype(jnp.bfloat16)
+        outs = jnp.einsum(
+            "erf,efd->erd", whole, w_down[picked], preferred_element_type=jnp.float32
+        ).astype(jnp.bfloat16)
+        mixed = jnp.einsum(
+            "wect,ewcd->wtd",
+            combine_table[:, picked],
+            outs.reshape(per_chunk, wide_count, CAP, feature_count),
+            preferred_element_type=jnp.float32,
         )
-    outs = jnp.concatenate(out_chunks, axis=0).reshape(
-        expert_count, wide_count, CAP, feature_count
-    )
-    mixed = jnp.einsum(
-        "wect,ewcd->wtd", combine_table, outs, preferred_element_type=jnp.float32
-    ).astype(jnp.bfloat16)
+        total = mixed if total is None else total + mixed
+    mixed = total.astype(jnp.bfloat16)
     back = jnp.argsort(order)
     mixed = lax.all_to_all(mixed[back], "wide", 0, 0)
     mixed = jnp.sum(mixed.astype(jnp.float32), axis=0)

time: 455 us -> 473 us (1.040)
  local copies, waits for them, and re-layouts: 83 us -> 92.4 us
  other arithmetic: 43.8 us -> 49.5 us
    ppermute x4, waiting for transfers between devices: 12.6 us -> 29.6 us  [local(): lax.ppermute(active, 'narrow', chip_pairs(chips - step))]
    ppermute x4, waiting for transfers between devices: 67.9 us -> 51.7 us  [local(): lax.ppermute(sent[:, :, (step - 1) * rows_own:step * rows_own], 'narrow',...]
    concatenate x1 -> x0, local copies, waits for them, and re-layouts: 8.61 us -> none  [local(): jnp.concatenate(out_chunks, axis=0)]
    convert_element_type x0 -> x4, local copies, waits for them, and re-layouts: none -> 7.9 us  [local(): outs = jnp.einsum('erf,efd->erd', whole, w_down[picked], preferred_elemen...]
    add x0 -> x2, other arithmetic: none -> 5.51 us  [local(): total = mixed if total is None else total + mixed]
    slice x1, local copies, waits for them, and re-layouts: 5.16 us -> 10.3 us  [local(): table[:, picked]]
    dot_general x1 -> x4, matrix products: 7.39 us -> 9.51 us  [local(): jnp.einsum('wect,ewcd->wtd', combine_table[:, picked], outs.reshape(per_c...]
    unnamed x66 -> x80, local copies, waits for them, and re-layouts: 26.5 us -> 28 us
  transfers between devices with their start and end apart: 18 -> 18, of which waited for: 8 -> 7; matrix products, arithmetic and copies ran while one was open for 22% -> 27% of each run, Pallas kernels for 0% -> 0%
where the time goes in v3:
time: 473 us; the launch traced here: 467 us
  blocking collectives  148 us (31%)
  local copies, waits for them, and re-layouts  92.4 us (20%)
  waiting for transfers between devices  81.4 us (17%)
  other arithmetic  49.5 us (10%)
  matrix products  46 us (10%)
  Pallas kernels  25.5 us (5%)
  between operations  14.7 us (3%)
  starting transfers between devices  9.92 us (2%)
    all_to_all x1, blocking collectives, local(): mixed = lax.all_to_all(mixed[back], 'wide', 0, 0)  57.3 us
    ppermute x4, waiting for transfers between devices, local(): lax.ppermute(sent[:, :, (step - 1) * rows_own:step * rows_own], 'narrow',...  51.7 us
    all_gather x1, blocking collectives, local(): lax.all_gather(jnp.sum(hidden * hidden, axis=1), ('wide', 'narrow'), axis=0)  40.5 us
    all_gather x1, blocking collectives, local(): lax.all_gather(routing, 'wide', axis=0)  32.2 us
    ppermute x4, waiting for transfers between devices, local(): lax.ppermute(active, 'narrow', chip_pairs(chips - step))  29.6 us
    unnamed x80, local copies, waits for them, and re-layouts  28 us
    pallas_call x1, Pallas kernels, attend(): pl.pallas_call(attend_kernel, grid=(reqs, groups), in_specs=[pl.BlockSpec...  25.5 us
    all_gather x1, blocking collectives, local(): stats = lax.all_gather(stats, 'narrow', axis=0)  18 us
  transfers between devices with their start and end apart: 18, of which 7 were waited for; matrix products, arithmetic and copies ran while one was open for 27% of the time, Pallas kernels for 0%

profile of v3, /device:TPU:0, one launch (start us, length us, event | category | flops | bytes accessed | tf_op | source)
XLA Modules:
  0.0 467.3 jit_solution(13550044214845000403)
XLA Ops:
  8.3 3.7 copy-done.2
  14.4 25.5 %shard_map.109 = (bf16[2,128,2304]{2,1,0:T(8,128)(2,1)S(1)}, f32[2,6,128,12]{3,2,1,0:T(8,128)S(1)}) custom-call(f32[2,1,512]{2,1,0:T(1,128)S(1)} %compare_convert_fusion.valid_ref, f32[128,32]{1,0:T(8,128)S(1)} %fusion.96.causal_ref, bf16[2,128,2304]{2,1,0:T(8,128)(2,1)S(1)} %copy-done.3, bf16[2,4,2,128,2304]{4,3,2,1,0:T(8,128)(2,1)S(1)} %copy-done.2, ...), custom_call_target="tpu_custom_call" | custom-call | tf_op jit(solution)/shard_map/pallas_call | solution.py:63
  42.3 3.4 copy.351
  45.7 4.2 all-to-all-start
  50.1 18.0 %all_gather.21 = f32[4,2,2,36,128]{4,2,3,1,0:T(2,128)S(1)} all-gather(f32[1,2,2,36,128]{4,2,3,1,0:T(2,128)S(1)} %bitcast.179), channel_id=1, replica_groups=mesh['wide'=8,'narrow'=4] {'narrow'}, dimensions={0}, use_global_device_ids=true | all-gather | bytes 368640 | tf_op jit(solution)/shard_map/all_gather | solution.py:131
  72.0 11.4 %copy.392 = bf16[8,576,2,720]{3,1,2,0:T(8,128)(2,1)} copy(bf16[8,576,2,720]{3,2,1,0:T(2,128)(2,1)} %param.20) | data formatting | bytes 26542080 | tf_op args[9]
  84.1 32.2 %all-gather.2 = f32[8192]{0:T(1024)S(1)} all-gather(f32[1024]{0:T(1024)S(1)} %pad_maximum_fusion.4), channel_id=4, replica_groups=mesh['wide'=8,'narrow'=4] {'wide'}, dimensions={0}, use_global_device_ids=true | all-gather | bytes 36864 | tf_op jit(solution)/shard_map/all_gather | solution.py:158
  121.5 7.1 %fusion = pred[8,640,256]{2,1,0:T(8,128)(4,1)} fusion(s32[8,256,2]{1,2,0:T(2,128)S(1)} %copy.299), kind=kLoop, calls=%fused_computation.7 | loop fusion | flops 3932160 | bytes 1327104 | tf_op jit(solution)/shard_map/reduce_or | solution.py:184
  128.6 10.3 %fusion.114 = (bf16[2,2,576,720]{3,2,0,1:T(8,128)(2,1)}, bf16[2,2,576,720]{3,2,0,1:T(8,128)(2,1)}, bf16[2,2,576,720]{3,2,0,1:T(8,128)(2,1)}, bf16[2,2,576,720]{3,2,0,1:T(8,128)(2,1)}) fusion(bf16[2,8,576,720]{3,2,0,1:T(8,128)(2,1)} %bitcast.155), kind=kLoop, calls=%fused_computation.177 | loop fusion | bytes 26542080 | tf_op jit(solution)/shard_map/slice | solution.py:212
  138.9 40.5 %all-gather.3 = f32[32,1,256]{2,1,0:T(1,128)S(1)} all-gather(f32[1,1,256]{2,1,0:T(1,128)S(1)} %bitcast.181), channel_id=3, replica_groups=mesh['wide'=8,'narrow'=4] {'wide','narrow'}, dimensions={0}, use_global_device_ids=true | all-gather | bytes 33792 | tf_op jit(solution)/shard_map/all_gather | solution.py:149
  186.0 3.6 convert_bitcast_fusion
  192.2 3.4 convert_bitcast_fusion.4
  199.7 3.4 convert_bitcast_fusion.2
  217.7 3.4 convert_bitcast_fusion.3
  224.6 3.6 convert_bitcast_fusion.1
  230.0 12.3 %collective-permute-done.13 = bf16[2,2,160,720]{3,2,1,0:T(8,128)(2,1)S(1)} collective-permute-done((bf16[2,2,160,720]{3,2,1,0:T(8,128)(2,1)S(1)}, bf16[2,2,160,720]{3,2,1,0:T(8,128)(2,1)S(1)}, u32[]{:S(2)}, u32[]{:S(2)}) %collective-permute-start.13) | collective-permute-done | bytes 921632 | tf_op jit(solution)/shard_map/ppermute | solution.py:224
  243.0 20.4 %collective-permute-done.10 = bf16[2,2,160,720]{3,2,1,0:T(8,128)(2,1)S(1)} collective-permute-done((bf16[2,2,160,720]{3,2,1,0:T(8,128)(2,1)S(1)}, bf16[2,2,160,720]{3,2,1,0:T(8,128)(2,1)S(1)}, u32[]{:S(2)}, u32[]{:S(2)}) %collective-permute-start.10) | collective-permute-done | bytes 921632 | tf_op jit(solution)/shard_map/ppermute | solution.py:224
  264.0 3.3 select_reduce_fusion
  269.6 4.4 collective-permute-done.14
  276.1 7.7 %collective-permute-done.11 = bf16[2,160,720]{2,1,0:T(8,128)(2,1)} collective-permute-done((bf16[2,160,720]{2,1,0:T(8,128)(2,1)S(1)}, bf16[2,160,720]{2,1,0:T(8,128)(2,1)}, u32[]{:S(2)}, u32[]{:S(2)}) %collective-permute-start.11) | collective-permute-done | bytes 460832 | tf_op jit(solution)/shard_map/ppermute | solution.py:230
  290.3 2.7 convert_add_fusion.2
  302.1 4.3 fusion.63
  308.3 4.2 convolution_bitcast_fusion
  314.2 4.5 fusion.58
  320.8 19.0 %collective-permute-done.7 = bf16[2,2,160,720]{3,2,1,0:T(8,128)(2,1)} collective-permute-done((bf16[2,2,160,720]{3,2,1,0:T(8,128)(2,1)}, bf16[2,2,160,720]{3,2,1,0:T(8,128)(2,1)}, u32[]{:S(2)}, u32[]{:S(2)}) %collective-permute-start.7) | collective-permute-done | bytes 921632 | tf_op jit(solution)/shard_map/ppermute | solution.py:224
  345.9 9.3 %collective-permute-done.8 = bf16[2,160,720]{2,1,0:T(8,128)(2,1)S(1)} collective-permute-done((bf16[2,160,720]{2,1,0:T(8,128)(2,1)S(1)}, bf16[2,160,720]{2,1,0:T(8,128)(2,1)S(1)}, u32[]{:S(2)}, u32[]{:S(2)}) %collective-permute-start.8) | collective-permute-done | bytes 460832 | tf_op jit(solution)/shard_map/ppermute | solution.py:230
  356.9 2.8 bitcast_add_fusion.2
  362.0 8.2 %collective-permute-done.3 = bf16[2,160,720]{2,1,0:T(8,128)(2,1)S(1)} collective-permute-done((bf16[2,160,720]{2,1,0:T(8,128)(2,1)S(1)}, bf16[2,160,720]{2,1,0:T(8,128)(2,1)S(1)}, u32[]{:S(2)}, u32[]{:S(2)}) %collective-permute-start.3) | collective-permute-done | bytes 460832 | tf_op jit(solution)/shard_map/ppermute | solution.py:230
  374.3 4.5 fusion.53
  383.1 2.8 bitcast_add_fusion.1
  387.5 4.3 fusion.48
  400.7 57.3 %all_to_all.10 = bf16[8,256,576]{1,2,0:T(8,128)(2,1)S(1)} all-to-all(bf16[8,256,576]{1,2,0:T(8,128)(2,1)S(1)} %gather_fusion.3), channel_id=1, replica_groups=mesh['wide'=8,'narrow'=4] {'wide'}, dimensions={0} | all-to-all | bytes 4718592 | tf_op jit(solution)/shard_map/all_to_all | solution.py:249
  (216 shorter events, 106.9 us)
Async XLA Ops:
  6.5 62.1 %copy-start = (bf16[256,2304]{1,0:T(8,128)(2,1)S(1)}, bf16[256,2304]{1,0:T(8,128)(2,1)}, u32[]{:S(2)}) copy-start(bf16[256,2304]{1,0:T(8,128)(2,1)} %param.16) | copy-start | bytes 3538948
  45.7 24.1 %all-to-all-start = ((bf16[4,256,576]{1,2,0:T(8,128)(2,1)}), bf16[4,256,576]{1,2,0:T(8,128)(2,1)S(1)}, u32[]{:S(2)}, u32[]{:S(2)}) async-start(bf16[4,256,576]{1,2,0:T(8,128)(2,1)} %bitcast.2), calls=%async_computation | async-start | bytes 2359296 | tf_op jit(solution)/shard_map/all_to_all | solution.py:135
  49.9 129.7 %all-gather.6.cloned.1.call-start = ((), (), s32[]{:S(2)}) async-start(), calls=%async_computation.2 | async-start | bytes 2654208 | tf_op jit(solution)/shard_map/all_gather | solution.py:150
  68.9 14.5 %copy-start.22 = (bf16[256,576]{0,1:T(8,128)(2,1)}, bf16[256,576]{0,1:T(8,128)(2,1)S(1)}, u32[]{:S(2)}) copy-start(bf16[256,576]{0,1:T(8,128)(2,1)S(1)} %copy.358) | copy-start | bytes 884740
  71.0 12.4 %copy-start.9 = (f32[256,576]{0,1:T(8,128)}, f32[256,576]{0,1:T(8,128)S(1)}, u32[]{:S(2)}) copy-start(f32[256,576]{0,1:T(8,128)S(1)} %multiply_reduce_fusion) | copy-start | bytes 1769476
  72.0 11.5 %copy-start.30 = (f32[256,2]{0,1:T(2,128)S(1)}, f32[256,2]{0,1:T(2,128)}, u32[]{:S(2)}) copy-start(f32[256,2]{0,1:T(2,128)} %param.19) | copy-start | bytes 6148
  72.0 11.8 %copy-start.31 = (s32[256,2]{0,1:T(2,128)S(1)}, s32[256,2]{0,1:T(2,128)}, u32[]{:S(2)}) copy-start(s32[256,2]{0,1:T(2,128)} %param.18) | copy-start | bytes 6148
  197.1 14.9 %collective-permute-start = (bf16[2,2,320,720]{3,2,1,0:T(8,128)(2,1)}, bf16[2,2,320,720]{3,2,1,0:T(8,128)(2,1)}, u32[]{:S(2)}, u32[]{:S(2)}) collective-permute-start(bf16[2,2,320,720]{3,2,1,0:T(8,128)(2,1)} %slice.211), channel_id=1, source_target_pairs={{0,1},{1,0},{2,3},{3,2},{4,5},{5,4},{6,7},{7,6},{8,9},{9,8},{10,11... | collective-permute-start | bytes 5529608 | tf_op jit(solution)/shard_map/ppermute | solution.py:214
  206.5 8.4 %collective-permute-start.5 = (bf16[2,2,320,720]{3,2,1,0:T(8,128)(2,1)}, bf16[2,2,320,720]{3,2,1,0:T(8,128)(2,1)}, u32[]{:S(2)}, u32[]{:S(2)}) collective-permute-start(bf16[2,2,320,720]{3,2,1,0:T(8,128)(2,1)} %slice.224), channel_id=1, source_target_pairs={{0,1},{1,0},{2,3},{3,2},{4,5},{5,4},{6,7},{7,6},{8,9},{9,8},{10,11... | collective-permute-start | bytes 5529608 | tf_op jit(solution)/shard_map/ppermute | solution.py:214
  217.6 24.7 %collective-permute-start.13 = (bf16[2,2,160,720]{3,2,1,0:T(8,128)(2,1)S(1)}, bf16[2,2,160,720]{3,2,1,0:T(8,128)(2,1)S(1)}, u32[]{:S(2)}, u32[]{:S(2)}) collective-permute-start(bf16[2,2,160,720]{3,2,1,0:T(8,128)(2,1)S(1)} %slice.314), channel_id=1, source_target_pairs={{0,2},{1,3},{2,0},{3,1},{4,6},{5,7},{6,4},{7,5},{8,10},{9,11},{10,... | collective-permute-start | bytes 2764808 | tf_op jit(solution)/shard_map/ppermute | solution.py:224
  221.2 7.1 %copy-start.11 = (bf16[2,2,640,720]{3,2,1,0:T(8,128)(2,1)}, bf16[2,2,640,720]{3,2,1,0:T(8,128)(2,1)S(1)}, u32[]{:S(2)}) copy-start(bf16[2,2,640,720]{3,2,1,0:T(8,128)(2,1)S(1)} %convert_bitcast_fusion.3) | copy-start | bytes 11059204
  221.3 69.0 %collective-permute-start.1 = (bf16[2,2,320,720]{3,2,1,0:T(8,128)(2,1)S(1)}, bf16[2,2,320,720]{3,2,1,0:T(8,128)(2,1)}, u32[]{:S(2)}, u32[]{:S(2)}) collective-permute-start(bf16[2,2,320,720]{3,2,1,0:T(8,128)(2,1)S(1)} %slice.215), channel_id=1, source_target_pairs={{0,1},{1,0},{2,3},{3,2},{4,5},{5,4},{6,7},{7,6},{8,9},{9,8},{10,11... | collective-permute-start | bytes 5529608 | tf_op jit(solution)/shard_map/ppermute | solution.py:214
  221.6 41.8 %collective-permute-start.10 = (bf16[2,2,160,720]{3,2,1,0:T(8,128)(2,1)S(1)}, bf16[2,2,160,720]{3,2,1,0:T(8,128)(2,1)S(1)}, u32[]{:S(2)}, u32[]{:S(2)}) collective-permute-start(bf16[2,2,160,720]{3,2,1,0:T(8,128)(2,1)S(1)} %slice.316), channel_id=1, source_target_pairs={{0,2},{1,3},{2,0},{3,1},{4,6},{5,7},{6,4},{7,5},{8,10},{9,11},{10,... | collective-permute-start | bytes 2764808 | tf_op jit(solution)/shard_map/ppermute | solution.py:224
  228.2 14.3 %copy-start.12 = (bf16[2,2,640,720]{3,2,1,0:T(8,128)(2,1)}, bf16[2,2,640,720]{3,2,1,0:T(8,128)(2,1)S(1)}, u32[]{:S(2)}) copy-start(bf16[2,2,640,720]{3,2,1,0:T(8,128)(2,1)S(1)} %convert_bitcast_fusion.1) | copy-start | bytes 11059204
  229.8 64.7 %collective-permute-start.6 = (bf16[2,2,320,720]{3,2,1,0:T(8,128)(2,1)}, bf16[2,2,320,720]{3,2,1,0:T(8,128)(2,1)}, u32[]{:S(2)}, u32[]{:S(2)}) collective-permute-start(bf16[2,2,320,720]{3,2,1,0:T(8,128)(2,1)} %slice.228), channel_id=1, source_target_pairs={{0,1},{1,0},{2,3},{3,2},{4,5},{5,4},{6,7},{7,6},{8,9},{9,8},{10,11... | collective-permute-start | bytes 5529608 | tf_op jit(solution)/shard_map/ppermute | solution.py:214
  242.9 31.1 %collective-permute-start.14 = (bf16[2,160,720]{2,1,0:T(8,128)(2,1)S(1)}, bf16[2,160,720]{2,1,0:T(8,128)(2,1)}, u32[]{:S(2)}, u32[]{:S(2)}) collective-permute-start(bf16[2,160,720]{2,1,0:T(8,128)(2,1)S(1)} %fusion.82), channel_id=1, source_target_pairs={{0,2},{1,3},{2,0},{3,1},{4,6},{5,7},{6,4},{7,5},{8,10},{9,11},{10,... | collective-permute-start | bytes 1382408 | tf_op jit(solution)/shard_map/ppermute | solution.py:230
  263.9 19.9 %collective-permute-start.11 = (bf16[2,160,720]{2,1,0:T(8,128)(2,1)S(1)}, bf16[2,160,720]{2,1,0:T(8,128)(2,1)}, u32[]{:S(2)}, u32[]{:S(2)}) collective-permute-start(bf16[2,160,720]{2,1,0:T(8,128)(2,1)S(1)} %fusion.84), channel_id=1, source_target_pairs={{0,2},{1,3},{2,0},{3,1},{4,6},{5,7},{6,4},{7,5},{8,10},{9,11},{10,... | collective-permute-start | bytes 1382408 | tf_op jit(solution)/shard_map/ppermute | solution.py:230
  276.1 24.4 %collective-permute-start.15 = (bf16[2,320,720]{2,1,0:T(8,128)(2,1)}, bf16[2,320,720]{2,1,0:T(8,128)(2,1)}, u32[]{:S(2)}, u32[]{:S(2)}) collective-permute-start(bf16[2,320,720]{2,1,0:T(8,128)(2,1)} %pad_maximum_fusion.3), channel_id=1, source_target_pairs={{0,1},{1,0},{2,3},{3,2},{4,5},{5,4},{6,7},{7,6},{8,9},{9,8},{10,11... | collective-permute-start | bytes 2764808 | tf_op jit(solution)/shard_map/ppermute | solution.py:233
  285.9 26.6 %collective-permute-start.12 = (bf16[2,320,720]{2,1,0:T(8,128)(2,1)}, bf16[2,320,720]{2,1,0:T(8,128)(2,1)}, u32[]{:S(2)}, u32[]{:S(2)}) collective-permute-start(bf16[2,320,720]{2,1,0:T(8,128)(2,1)} %pad_maximum_fusion.2), channel_id=1, source_target_pairs={{0,1},{1,0},{2,3},{3,2},{4,5},{5,4},{6,7},{7,6},{8,9},{9,8},{10,11... | collective-permute-start | bytes 2764808 | tf_op jit(solution)/shard_map/ppermute | solution.py:233
  294.2 49.3 %collective-permute-start.2 = (bf16[2,2,160,720]{3,2,1,0:T(8,128)(2,1)}, bf16[2,2,160,720]{3,2,1,0:T(8,128)(2,1)}, u32[]{:S(2)}, u32[]{:S(2)}) collective-permute-start(bf16[2,2,160,720]{3,2,1,0:T(8,128)(2,1)} %slice.315), channel_id=1, source_target_pairs={{0,2},{1,3},{2,0},{3,1},{4,6},{5,7},{6,4},{7,5},{8,10},{9,11},{10,... | collective-permute-start | bytes 2764808 | tf_op jit(solution)/shard_map/ppermute | solution.py:224
  296.7 5.4 %copy-start.25 = (bf16[2,160,720]{1,2,0:T(8,128)(2,1)S(1)}, bf16[2,160,720]{1,2,0:T(8,128)(2,1)}, u32[]{:S(2)}) copy-start(bf16[2,160,720]{1,2,0:T(8,128)(2,1)} %copy.314) | copy-start | bytes 1382404
  296.7 5.4 %copy-start.27 = (bf16[2,160,720]{1,2,0:T(8,128)(2,1)S(1)}, bf16[2,160,720]{1,2,0:T(8,128)(2,1)}, u32[]{:S(2)}) copy-start(bf16[2,160,720]{1,2,0:T(8,128)(2,1)} %copy.315) | copy-start | bytes 1382404
  298.9 40.9 %collective-permute-start.7 = (bf16[2,2,160,720]{3,2,1,0:T(8,128)(2,1)}, bf16[2,2,160,720]{3,2,1,0:T(8,128)(2,1)}, u32[]{:S(2)}, u32[]{:S(2)}) collective-permute-start(bf16[2,2,160,720]{3,2,1,0:T(8,128)(2,1)} %slice.313), channel_id=1, source_target_pairs={{0,2},{1,3},{2,0},{3,1},{4,6},{5,7},{6,4},{7,5},{8,10},{9,11},{10,... | collective-permute-start | bytes 2764808 | tf_op jit(solution)/shard_map/ppermute | solution.py:224
  308.3 5.9 %copy-start.24 = (bf16[2,160,720]{1,2,0:T(8,128)(2,1)S(1)}, bf16[2,160,720]{1,2,0:T(8,128)(2,1)}, u32[]{:S(2)}) copy-start(bf16[2,160,720]{1,2,0:T(8,128)(2,1)} %copy.319) | copy-start | bytes 1382404
  342.2 12.9 %collective-permute-start.8 = (bf16[2,160,720]{2,1,0:T(8,128)(2,1)S(1)}, bf16[2,160,720]{2,1,0:T(8,128)(2,1)S(1)}, u32[]{:S(2)}, u32[]{:S(2)}) collective-permute-start(bf16[2,160,720]{2,1,0:T(8,128)(2,1)S(1)} %fusion.86), channel_id=1, source_target_pairs={{0,2},{1,3},{2,0},{3,1},{4,6},{5,7},{6,4},{7,5},{8,10},{9,11},{10,... | collective-permute-start | bytes 1382408 | tf_op jit(solution)/shard_map/ppermute | solution.py:230
  342.6 14.3 %slice-start.2 = ((s8[4718592]{0:T(1024)(128)(4,1)}), s8[4194304]{0:T(1024)(128)(4,1)S(1)}, s32[]{:S(2)}) async-start(s8[4718592]{0:T(1024)(128)(4,1)} %bitcast.162), calls=%async_computation.5 | async-start | bytes 8388608
  343.5 13.3 %slice-start.3 = ((s8[4718592]{0:T(1024)(128)(4,1)}), s8[524288]{0:T(1024)(128)(4,1)S(1)}, s32[]{:S(2)}) async-start(s8[4718592]{0:T(1024)(128)(4,1)} %bitcast.162), calls=%async_computation.6 | async-start | bytes 1048576
  356.2 17.3 %collective-permute-start.9 = (bf16[2,320,720]{2,1,0:T(8,128)(2,1)}, bf16[2,320,720]{2,1,0:T(8,128)(2,1)S(1)}, u32[]{:S(2)}, u32[]{:S(2)}) collective-permute-start(bf16[2,320,720]{2,1,0:T(8,128)(2,1)} %pad_maximum_fusion.1), channel_id=1, source_target_pairs={{0,1},{1,0},{2,3},{3,2},{4,5},{5,4},{6,7},{7,6},{8,9},{9,8},{10,11... | collective-permute-start | bytes 2764808 | tf_op jit(solution)/shard_map/ppermute | solution.py:233
  356.5 13.7 %collective-permute-start.3 = (bf16[2,160,720]{2,1,0:T(8,128)(2,1)S(1)}, bf16[2,160,720]{2,1,0:T(8,128)(2,1)S(1)}, u32[]{:S(2)}, u32[]{:S(2)}) collective-permute-start(bf16[2,160,720]{2,1,0:T(8,128)(2,1)S(1)} %fusion.88), channel_id=1, source_target_pairs={{0,2},{1,3},{2,0},{3,1},{4,6},{5,7},{6,4},{7,5},{8,10},{9,11},{10,... | collective-permute-start | bytes 1382408 | tf_op jit(solution)/shard_map/ppermute | solution.py:230
  371.2 14.6 %collective-permute-start.4 = (bf16[2,320,720]{2,1,0:T(8,128)(2,1)}, bf16[2,320,720]{2,1,0:T(8,128)(2,1)}, u32[]{:S(2)}, u32[]{:S(2)}) collective-permute-start(bf16[2,320,720]{2,1,0:T(8,128)(2,1)} %pad_maximum_fusion), channel_id=1, source_target_pairs={{0,1},{1,0},{2,3},{3,2},{4,5},{5,4},{6,7},{7,6},{8,9},{9,8},{10,11... | collective-permute-start | bytes 2764808 | tf_op jit(solution)/shard_map/ppermute | solution.py:233
  383.1 4.4 copy-start.28
  400.7 59.3 %copy-start.1 = (bf16[256,2304]{1,0:T(8,128)(2,1)S(1)}, bf16[256,2304]{1,0:T(8,128)(2,1)}, u32[]{:S(2)}) copy-start(bf16[256,2304]{1,0:T(8,128)(2,1)} %param.16) | copy-start | bytes 3538948
  (24 other events, 65.7 us)
Sparse Core Ops, SparseCore 0:
  72.1 54.9 all-gather.5
